TPU v7x, 128 devices: a whole 4x4x4 slice. The times are simulated.
128 devices in a mesh: rep: 8 (over z, y_hi), slab: 16 (over y_lo, x, core).
Axes of the slice: x: 4, y: 4 (y_hi: 2, y_lo: 2; y = y_hi * 2 + y_lo), z: 4, core: 2. Of those that a mesh axis runs over, the one named last changes fastest.
Arguments:
- feats: bfloat16 [8, 32, 24576], P('rep', None, 'slab'), may hold values from -6 to 6
- tile_weight: bfloat16 [8, 1536, 64, 512], P('rep', 'slab'), may hold values from -0.25 to 0.25
- tile_atom: int32 [8, 1536], P('rep', 'slab'), may hold values from 0 to 23
- tile_cell: int32 [8, 1536], P('rep', 'slab'), may hold values from 0 to 31
- tile_live: int32 [8, 16], P('rep', 'slab'), may hold values from 24 to 96, as said below
- w_mix: bfloat16 [32, 32], replicated, may hold values from -1 to 1
- conv_w: bfloat16 [27, 32, 32], replicated, may hold values from -0.21875 to 0.21875
- cotangent: bfloat16 [8, 32, 24576], P('rep', None, 'slab'), may hold values from -6 to 6
Outputs:
- potential: bfloat16 [8, 32, 24576], P('rep', None, 'slab')
- grad_feats: bfloat16 [8, 32, 24576], P('rep', None, 'slab')
- grad_conv: float32 [27, 32, 32], replicated
- grad_mix: float32 [32, 32], replicated
Inputs may be any that keep to these rules, and one draw needn't show every extreme that they name: The first tile_live slots of a slab's list are live, the rest are ignored; in every system some slab has all 96 slots live. `tile_atom`: atom block within the tile's own slab. `tile_cell`: cell block within the slab's window of 8 planes that starts 2 planes below the slab.
All inputs are finite; a program needn't handle non-finite values.
Results may differ from a plain program's by a relative error of at most 0.013.
Values may be sent and summed in bfloat16 or wider, within the bound.
A program may use at most 128 MiB of HBM per device.

v0:
```python
import math

import jax
import jax.numpy as jnp
from jax import lax
from jax.sharding import PartitionSpec as P

C = 32
GY = 32
GX = 64
ZD = 4
ZH = 2
A_DEV = 1536
TILE_A = 64
TILE_C = 512
PW = 8
NB = 32
NAB = 24


def from_behind(value, axis, steps):
    count = lax.axis_size(axis)
    pairs = [(source, (source + steps) % count) for source in range(count)]
    return lax.ppermute(value, axis, pairs)


def extended_2(block, sides, width):
    for axis, dim in sides:
        count = lax.axis_size(axis)
        forward = [(i, i + 1) for i in range(count - 1)]
        forward.append((count - 1, 0))
        backward = [(target, source) for source, target in forward]
        low = lax.ppermute(
            lax.slice_in_dim(block, block.shape[dim] - width, None, axis=dim), axis, forward
        )
        high = lax.ppermute(lax.slice_in_dim(block, 0, width, axis=dim), axis, backward)
        block = jnp.concatenate([low, block, high], axis=dim)
    return block


def shifted_stack(field):
    planes = field.shape[1]
    shaped = field.reshape(C, planes, GY, GX)
    pieces = []
    for row_off in (-1, 0, 1):
        for col_off in (-1, 0, 1):
            rolled = jnp.roll(shaped, (-row_off, -col_off), (2, 3))
            pieces.append(rolled.reshape(C, planes, GY * GX))
    return jnp.concatenate(pieces, axis=0)


def conv_valid(field, kernel_set):
    planes = field.shape[1] - 2
    stacked = shifted_stack(field)
    result = jnp.zeros((C, planes, GY * GX), jnp.float32)
    for plane_off in range(3):
        kernel = jnp.transpose(kernel_set[plane_off * 9 : (plane_off + 1) * 9], (1, 0, 2)).reshape(
            C, 9 * C
        )
        result = result + jnp.einsum(
            "ok,kpn->opn",
            kernel,
            stacked[:, plane_off : plane_off + planes],
            preferred_element_type=jnp.float32,
        )
    return result


def weight_grad(upstream, field):
    planes = upstream.shape[1]
    stacked = shifted_stack(field)
    collected = []
    for plane_off in range(3):
        product = jnp.einsum(
            "opn,kpn->ok",
            upstream,
            stacked[:, plane_off : plane_off + planes],
            preferred_element_type=jnp.float32,
        )
        collected.append(jnp.transpose(product.reshape(C, 9, C), (1, 0, 2)))
    return jnp.concatenate(collected, axis=0)


def deposit_tiles(source, weights, atom_ids, first_tile, live_tiles):
    blocks = source.reshape(C, NAB, TILE_A)
    picked = jnp.take(blocks, atom_ids, axis=1)
    product = jnp.einsum("ctk,tkn->tcn", picked, weights, preferred_element_type=jnp.float32)
    alive = first_tile + jnp.arange(weights.shape[0], dtype=jnp.int32) < live_tiles
    return jnp.where(alive[:, None, None], product, 0.0)


def collect_tiles(window_blocks, weights, cell_ids, first_tile, live_tiles):
    picked = jnp.take(window_blocks, cell_ids, axis=1)
    product = jnp.einsum("ctn,tkn->tck", picked, weights, preferred_element_type=jnp.float32)
    alive = first_tile + jnp.arange(weights.shape[0], dtype=jnp.int32) < live_tiles
    return jnp.where(alive[:, None, None], product, 0.0)


def over_tiles(tile_fn, operand, weights, source_ids, target_ids, live_tiles, segments):
    products = tile_fn(operand, weights, source_ids, 0, live_tiles)
    return jax.ops.segment_sum(products, target_ids, num_segments=segments)


def fold_rims(window):
    upper_rim = window[:, ZH + ZD :]
    lower_rim = window[:, :ZH]
    from_below = from_behind(upper_rim.astype(jnp.bfloat16), "slab", 1).astype(upper_rim.dtype)
    from_above = from_behind(lower_rim.astype(jnp.bfloat16), "slab", -1).astype(lower_rim.dtype)
    owned = window[:, ZH : ZH + ZD]
    owned = owned.at[:, :ZH].add(from_below)
    owned = owned.at[:, ZD - ZH :].add(from_above)
    return owned


def with_near(field):
    return extended_2(field, (("slab", 1),), 1)


def with_read(field):
    return extended_2(field, (("slab", 1),), ZH)


def local(feats, tile_weight, tile_atom, tile_cell, tile_live, w_mix, conv_w, cotangent):
    atom_feats = feats[0]
    weights = tile_weight[0]
    atom_ids = tile_atom[0]
    cell_ids = tile_cell[0]
    live_tiles = tile_live[0, 0]
    kernel_flip = jnp.transpose(conv_w[::-1], (0, 2, 1))

    def spread_mesh(source):
        sums = over_tiles(deposit_tiles, source, weights, atom_ids, cell_ids, live_tiles, NB)
        window = jnp.transpose(sums, (1, 0, 2)).reshape(C, PW, GY * GX)
        return fold_rims(window)

    def gather_atoms(extended):
        window_blocks = extended.reshape(C, NB, TILE_C)
        sums = over_tiles(
            collect_tiles, window_blocks, weights, cell_ids, atom_ids, live_tiles, NAB
        )
        return jnp.transpose(sums, (1, 0, 2)).reshape(C, A_DEV)

    mixed = jnp.dot(w_mix, atom_feats, preferred_element_type=jnp.float32).astype(jnp.bfloat16)
    density = spread_mesh(mixed).astype(jnp.bfloat16)
    density_near = with_near(density)
    field_mesh = with_read(conv_valid(density_near, conv_w).astype(jnp.bfloat16))
    potential = gather_atoms(field_mesh).astype(jnp.bfloat16)
    mesh_grad = spread_mesh(cotangent[0]).astype(jnp.bfloat16)
    density_grad = with_read(conv_valid(with_near(mesh_grad), kernel_flip).astype(jnp.bfloat16))
    mixed_grad = gather_atoms(density_grad).astype(jnp.bfloat16)
    feats_grad = jnp.dot(w_mix.T, mixed_grad, preferred_element_type=jnp.float32).astype(
        jnp.bfloat16
    )
    conv_part = weight_grad(mesh_grad, density_near)
    mix_part = lax.dot_general(
        mixed_grad, atom_feats, (((1,), (1,)), ((), ())), preferred_element_type=jnp.float32
    )
    conv_total, mix_total = lax.psum((conv_part, mix_part), ("rep", "slab"))
    groups = lax.axis_size("rep") * lax.axis_size("slab")
    conv_scale = math.sqrt(groups * ZD * GY * GX)
    mix_scale = math.sqrt(groups * A_DEV)
    return (potential[None], feats_grad[None], conv_total / conv_scale, mix_total / mix_scale)


def solution(mesh):
    return jax.shard_map(
        local,
        mesh=mesh,
        in_specs=(
            P("rep", None, "slab"),
            P("rep", "slab", None, None),
            P("rep", "slab"),
            P("rep", "slab"),
            P("rep", "slab"),
            P(),
            P(),
            P("rep", None, "slab"),
        ),
        out_specs=(P("rep", None, "slab"), P("rep", None, "slab"), P(), P()),
        check_vma=False,
    )
```

profile of v0, /device:TPU:1, one launch (start us, length us, event | category | flops | bytes accessed | tf_op | source)
XLA Modules:
  0.0 452.8 jit_solution(4543794386522970593)
XLA Ops:
  11.0 6.5 %broadcast_select_fusion.1 = f32[96,32,512]{2,1,0:T(8,128)} fusion(pred[96]{0:T(512)(128)(4,1)S(1)} %iota_compare_fusion, bf16[1,96,64,512]{3,2,1,0:T(8,128)(2,1)} %param.21, bf16[96,32,64]{2,1,0:T(8,128)(2,1)S(1)} %gather_fusion, pred[96]{0:T(512)(128)(4,1)S(1)} %get-tuple-element.115), kind=kOutput, calls=%fused_computation.47 | convolution fusion | flops 203096064 | bytes 12976320 | tf_op jit(solution)/shard_map/ctk,tkn->tcn/dot_general | solution.py:87
  18.2 12.9 %scatter_fusion = f32[32,32,512]{2,1,0:T(8,128)S(1)} fusion(f32[32,32,512]{2,1,0:T(8,128)S(1)} %broadcast.79.clone, s32[96]{0:T(128)S(1)} %bitcast.209, f32[96,32,512]{2,1,0:T(8,128)} %broadcast_select_fusion.1), kind=kCustom, calls=%fused_computation.4 | custom fusion | flops 1572864 | bytes 18874752 | tf_op jit(solution)/shard_map/scatter-add | solution.py:101
  31.2 2.6 copy.46
  33.7 2.2 reshape.262
  38.1 2.6 collective-permute-start
  41.8 6.5 %broadcast_select_fusion = f32[96,32,512]{2,1,0:T(8,128)} fusion(pred[96]{0:T(512)(128)(4,1)S(1)} %iota_compare_fusion, bf16[1,96,64,512]{3,2,1,0:T(8,128)(2,1)} %param.21, bf16[96,32,64]{2,1,0:T(8,128)(2,1)S(1)} %gather_fusion.2, pred[96]{0:T(512)(128)(4,1)S(1)} %get-tuple-element.115), kind=kOutput, calls=%fused_computation.46 | convolution fusion | flops 203096064 | bytes 12976320 | tf_op jit(solution)/shard_map/ctk,tkn->tcn/dot_general | solution.py:87
  48.6 12.9 %scatter_fusion.2 = f32[32,32,512]{2,1,0:T(8,128)S(1)} fusion(f32[32,32,512]{2,1,0:T(8,128)S(1)} %broadcast.79.clone.1, s32[96]{0:T(128)S(1)} %bitcast.210, f32[96,32,512]{2,1,0:T(8,128)} %broadcast_select_fusion), kind=kCustom, calls=%fused_computation.6 | custom fusion | flops 1572864 | bytes 18874752 | tf_op jit(solution)/shard_map/scatter-add | solution.py:101
  61.5 2.6 copy.60
  64.1 2.2 reshape.276
  80.1 3.1 collective-permute-start.3
  85.1 4.0 collective-permute-start.9
  93.1 2.5 fusion.39
  95.6 2.3 fusion.40
  97.9 2.6 fusion.44
  100.5 2.6 fusion.43
  105.0 2.4 fusion.82
  107.4 2.5 fusion.83
  110.4 2.0 pad_maximum_fusion.9
  112.4 2.8 reshape.271
  115.2 3.9 pad_maximum_fusion.8
  119.2 3.9 reshape.269
  123.1 3.9 pad_maximum_fusion.5
  126.9 3.5 reshape.266
  130.5 3.5 reshape.265
  134.0 3.9 pad_maximum_fusion.4
  137.9 3.5 reshape.264
  141.5 2.2 constant_dynamic-update-slice_fusion.8
  143.7 3.4 pad_maximum_fusion.6
  147.1 3.5 reshape.267
  150.7 3.9 pad_maximum_fusion.7
  154.6 3.5 reshape.268
  158.1 2.2 reshape.270
  160.3 2.2 constant_dynamic-update-slice_fusion.7
  169.3 3.8 fusion.12
  173.1 3.7 fusion.10
  181.9 2.6 fusion.32
  184.6 2.6 fusion.31
  188.9 2.4 fusion.78
  191.4 2.4 fusion.79
  193.8 2.6 fusion.36
  196.3 2.7 fusion.35
  200.7 4.0 pad_maximum_fusion.15
  204.7 2.8 reshape.285
  207.5 3.5 reshape.284
  211.0 4.0 pad_maximum_fusion.14
  215.0 3.5 reshape.283
  218.5 3.9 pad_maximum_fusion.13
  222.4 3.5 reshape.282
  226.0 3.9 pad_maximum_fusion.12
  229.9 3.5 reshape.281
  233.4 3.9 pad_maximum_fusion.11
  237.4 3.5 reshape.280
  242.9 2.7 pad_maximum_fusion.10
  245.7 2.4 reshape.278
  257.9 3.9 collective-permute-start.11
  266.3 3.8 collective-permute-start.5
  270.1 76.9 %all-reduce.2.cloned.1.call-done = f32[27,32,32]{1,2,0:T(8,128)} async-done(((f32[27,32,32]{1,2,0:T(8,128)}), f32[27,32,32]{1,2,0:T(8,128)}) %all-reduce.2.cloned.1.call-update) | async-done | bytes 110608 | tf_op jit(solution)/shard_map/psum | solution.py:158
  351.1 2.5 gather_fusion.3
  353.6 5.6 %fusion.52 = f32[96,32,64]{2,1,0:T(8,128)S(1)} fusion(bf16[1,96,64,512]{3,2,1,0:T(8,128)(2,1)} %param.21, bf16[96,32,512]{2,1,0:T(8,128)(2,1)} %gather_fusion.3, pred[96]{0:T(512)(128)(4,1)S(1)} %get-tuple-element.114, pred[96]{0:T(512)(128)(4,1)S(1)} %iota_compare_fusion), kind=kOutput, calls=%fused_computation.92 | convolution fusion | flops 203096064 | bytes 10223808 | tf_op jit(solution)/shard_map/ctn,tkn->tck/dot_general | solution.py:94
  359.3 4.5 scatter_fusion.3
  365.1 63.5 %psum.15 = f32[32,32]{1,0:T(8,128)S(1)} all-reduce(f32[32,32]{1,0:T(8,128)S(1)} %fusion.69), channel_id=1, replica_groups=mesh['rep'=8,'slab'=16] {'rep','slab'}, use_global_device_ids=true, to_apply=%region_5.8 | all-reduce | flops 1024 | bytes 8192 | tf_op jit(solution)/shard_map/psum | solution.py:158
  432.2 2.5 gather_fusion.1
  434.7 5.6 %fusion.47 = f32[96,32,64]{2,1,0:T(8,128)S(1)} fusion(bf16[1,96,64,512]{3,2,1,0:T(8,128)(2,1)} %param.21, bf16[96,32,512]{2,1,0:T(8,128)(2,1)} %gather_fusion.1, pred[96]{0:T(512)(128)(4,1)S(1)} %get-tuple-element.114, pred[96]{0:T(512)(128)(4,1)S(1)} %iota_compare_fusion), kind=kOutput, calls=%fused_computation.91 | convolution fusion | flops 203096064 | bytes 10223808 | tf_op jit(solution)/shard_map/ctn,tkn->tck/dot_general | solution.py:94
  440.3 4.5 scatter_fusion.1
  (192 shorter events, 70.5 us)
Async XLA Ops:
  7.2 2.1 copy-start
  7.2 339.8 %all-reduce.2.cloned.1.call-start = ((), (), s32[]{:S(2)}) async-start(), calls=%async_computation | async-start | bytes 884736 | tf_op jit(solution)/shard_map/psum | solution.py:158
  17.6 0.7 copy-start.32
  35.9 1.4 copy-start.2
  35.9 5.0 %copy-start.30 = (bf16[1,32,1536]{2,1,0:T(8,128)(2,1)S(1)}, bf16[1,32,1536]{2,1,0:T(8,128)(2,1)}, u32[]{:S(2)}) copy-start(bf16[1,32,1536]{2,1,0:T(8,128)(2,1)} %param.27) | copy-start | bytes 294916
  38.1 39.7 %collective-permute-start = (bf16[32,2,2048]{2,0,1:T(8,128)(2,1)}, bf16[32,2,2048]{2,0,1:T(8,128)(2,1)S(1)}, u32[]{:S(2)}, u32[]{:S(2)}) collective-permute-start(bf16[32,2,2048]{2,0,1:T(8,128)(2,1)} %get-tuple-element.97), channel_id=1, source_target_pairs={{0,1},{1,2},{2,3},{3,4},{4,5},{5,6},{6,7},{7,8},{8,9},{9,10},{10,1... | collective-permute-start | bytes 786440 | tf_op jit(solution)/shard_map/ppermute | solution.py:24
  40.7 38.2 %collective-permute-start.1 = (bf16[32,2,2048]{2,0,1:T(8,128)(2,1)}, bf16[32,2,2048]{2,0,1:T(8,128)(2,1)S(1)}, u32[]{:S(2)}, u32[]{:S(2)}) collective-permute-start(bf16[32,2,2048]{2,0,1:T(8,128)(2,1)} %get-tuple-element.96), channel_id=1, source_target_pairs={{0,15},{1,0},{2,1},{3,2},{4,3},{5,4},{6,5},{7,6},{8,7},{9,8},{10,9... | collective-permute-start | bytes 786440 | tf_op jit(solution)/shard_map/ppermute | solution.py:24
  66.3 4.6 %copy-start.19 = (bf16[27,32,32]{2,1,0:T(8,128)(2,1)S(1)}, bf16[27,32,32]{2,1,0:T(8,128)(2,1)}, u32[]{:S(2)}) copy-start(bf16[27,32,32]{2,1,0:T(8,128)(2,1)} %param.26) | copy-start | bytes 165892
  66.3 4.7 %copy-start.3 = (f32[32,8,2048]{2,1,0:T(8,128)S(1)}, f32[32,8,2048]{2,1,0:T(8,128)}, u32[]{:S(2)}) copy-start(f32[32,8,2048]{2,1,0:T(8,128)} %copy-done.2) | copy-start | bytes 6291460
  68.3 14.9 %collective-permute-start.6 = (bf16[32,2,2048]{2,0,1:T(8,128)(2,1)}, bf16[32,2,2048]{2,0,1:T(8,128)(2,1)}, u32[]{:S(2)}, u32[]{:S(2)}) collective-permute-start(bf16[32,2,2048]{2,0,1:T(8,128)(2,1)} %get-tuple-element.95), channel_id=1, source_target_pairs={{0,1},{1,2},{2,3},{3,4},{4,5},{5,6},{6,7},{7,8},{8,9},{9,10},{10,1... | collective-permute-start | bytes 786440 | tf_op jit(solution)/shard_map/ppermute | solution.py:24
  70.0 14.2 %collective-permute-start.7 = (bf16[32,2,2048]{2,0,1:T(8,128)(2,1)}, bf16[32,2,2048]{2,0,1:T(8,128)(2,1)S(1)}, u32[]{:S(2)}, u32[]{:S(2)}) collective-permute-start(bf16[32,2,2048]{2,0,1:T(8,128)(2,1)} %get-tuple-element.94), channel_id=1, source_target_pairs={{0,15},{1,0},{2,1},{3,2},{4,3},{5,4},{6,5},{7,6},{8,7},{9,8},{10,9... | collective-permute-start | bytes 786440 | tf_op jit(solution)/shard_map/ppermute | solution.py:24
  72.3 1.4 copy-start.6
  73.6 1.3 copy-start.4
  73.6 4.2 slice-start.3
  78.9 4.3 copy-start.5
  79.0 4.3 slice-start.2
  79.2 9.9 %collective-permute-start.2 = (bf16[32,1,2048]{2,0,1:T(8,128)(2,1)S(1)}, bf16[32,1,2048]{2,0,1:T(8,128)(2,1)S(1)}, u32[]{:S(2)}, u32[]{:S(2)}) collective-permute-start(bf16[32,1,2048]{2,0,1:T(8,128)(2,1)S(1)} %get-tuple-element.104), channel_id=1, source_target_pairs={{0,1},{1,2},{2,3},{3,4},{4,5},{5,6},{6,7},{7,8},{8,9},{9,10},{10,1... | collective-permute-start | bytes 393224 | tf_op jit(solution)/shard_map/ppermute | solution.py:33
  80.1 9.0 %collective-permute-start.3 = (bf16[32,1,2048]{2,0,1:T(8,128)(2,1)S(1)}, bf16[32,1,2048]{2,0,1:T(8,128)(2,1)S(1)}, u32[]{:S(2)}, u32[]{:S(2)}) collective-permute-start(bf16[32,1,2048]{2,0,1:T(8,128)(2,1)S(1)} %get-tuple-element.105), channel_id=1, source_target_pairs={{1,0},{2,1},{3,2},{4,3},{5,4},{6,5},{7,6},{8,7},{9,8},{10,9},{11,1... | collective-permute-start | bytes 393224 | tf_op jit(solution)/shard_map/ppermute | solution.py:36
  85.1 93.1 %collective-permute-start.8 = (bf16[32,1,2048]{2,0,1:T(8,128)(2,1)}, bf16[32,1,2048]{2,0,1:T(8,128)(2,1)}, u32[]{:S(2)}, u32[]{:S(2)}) collective-permute-start(bf16[32,1,2048]{2,0,1:T(8,128)(2,1)} %get-tuple-element.100), channel_id=1, source_target_pairs={{0,1},{1,2},{2,3},{3,4},{4,5},{5,6},{6,7},{7,8},{8,9},{9,10},{10,1... | collective-permute-start | bytes 393224 | tf_op jit(solution)/shard_map/ppermute | solution.py:33
  85.1 93.1 %collective-permute-start.9 = (bf16[32,1,2048]{2,0,1:T(8,128)(2,1)}, bf16[32,1,2048]{2,0,1:T(8,128)(2,1)}, u32[]{:S(2)}, u32[]{:S(2)}) collective-permute-start(bf16[32,1,2048]{2,0,1:T(8,128)(2,1)} %get-tuple-element.101), channel_id=1, source_target_pairs={{1,0},{2,1},{3,2},{4,3},{5,4},{6,5},{7,6},{8,7},{9,8},{10,9},{11,1... | collective-permute-start | bytes 393224 | tf_op jit(solution)/shard_map/ppermute | solution.py:36
  89.1 0.6 copy-start.20
  89.8 0.7 copy-start.22
  141.5 2.2 copy-start.7
  160.3 2.3 copy-start.12
  160.3 3.2 copy-start.16
  162.5 1.9 copy-start.21
  162.5 1.9 copy-start.23
  163.5 1.9 copy-start.15
  164.5 1.9 copy-start.9
  165.4 1.9 copy-start.14
  169.3 7.6 %copy-start.1 = (bf16[288,6,2048]{2,0,1:T(8,128)(2,1)S(1)}, bf16[288,6,2048]{2,0,1:T(8,128)(2,1)}, u32[]{:S(2)}) copy-start(bf16[288,6,2048]{2,0,1:T(8,128)(2,1)} %constant_dynamic-update-slice_fusion) | copy-start | bytes 21233668
  248.1 1.4 copy-start.18
  248.1 1.6 copy-start.17
  249.5 1.2 copy-start.13
  250.7 1.3 copy-start.11
  250.7 1.4 copy-start.10
  251.9 1.2 copy-start.8
  253.1 0.9 copy-start.24
  254.0 1.2 copy-start.27
  255.2 1.3 copy-start.26
  255.2 6.6 %slice-start = ((s8[7077888]{0:T(1024)(128)(4,1)}), s8[4194304]{0:T(1024)(128)(4,1)S(1)}, s32[]{:S(2)}) async-start(s8[7077888]{0:T(1024)(128)(4,1)} %bitcast.196), calls=%async_computation.1 | async-start | bytes 8388608
  256.5 5.3 %slice-start.1 = ((s8[7077888]{0:T(1024)(128)(4,1)}), s8[2883584]{0:T(1024)(128)(4,1)S(1)}, s32[]{:S(2)}) async-start(s8[7077888]{0:T(1024)(128)(4,1)} %bitcast.196), calls=%async_computation.2 | async-start | bytes 5767168
  256.5 5.3 %copy-start.25 = (bf16[32,9,32]{0,2,1:T(8,128)(2,1)S(1)}, bf16[32,9,32]{0,2,1:T(8,128)(2,1)}, u32[]{:S(2)}) copy-start(bf16[32,9,32]{0,2,1:T(8,128)(2,1)} %copy.50) | copy-start | bytes 55300
  257.8 91.1 %collective-permute-start.10 = (bf16[32,2,2048]{2,0,1:T(8,128)(2,1)S(1)}, bf16[32,2,2048]{2,0,1:T(8,128)(2,1)S(1)}, u32[]{:S(2)}, u32[]{:S(2)}) collective-permute-start(bf16[32,2,2048]{2,0,1:T(8,128)(2,1)S(1)} %get-tuple-element.98), channel_id=1, source_target_pairs={{0,1},{1,2},{2,3},{3,4},{4,5},{5,6},{6,7},{7,8},{8,9},{9,10},{10,1... | collective-permute-start | bytes 786440 | tf_op jit(solution)/shard_map/ppermute | solution.py:33
  257.9 91.1 %collective-permute-start.11 = (bf16[32,2,2048]{2,0,1:T(8,128)(2,1)S(1)}, bf16[32,2,2048]{2,0,1:T(8,128)(2,1)S(1)}, u32[]{:S(2)}, u32[]{:S(2)}) collective-permute-start(bf16[32,2,2048]{2,0,1:T(8,128)(2,1)S(1)} %get-tuple-element.99), channel_id=1, source_target_pairs={{1,0},{2,1},{3,2},{4,3},{5,4},{6,5},{7,6},{8,7},{9,8},{10,9},{11,1... | collective-permute-start | bytes 786440 | tf_op jit(solution)/shard_map/ppermute | solution.py:36
  261.8 1.2 copy-start.28
  263.1 1.2 copy-start.29
  266.3 162.9 %collective-permute-start.4 = (bf16[32,2,2048]{2,0,1:T(8,128)(2,1)}, bf16[32,2,2048]{2,0,1:T(8,128)(2,1)}, u32[]{:S(2)}, u32[]{:S(2)}) collective-permute-start(bf16[32,2,2048]{2,0,1:T(8,128)(2,1)} %get-tuple-element.102), channel_id=1, source_target_pairs={{0,1},{1,2},{2,3},{3,4},{4,5},{5,6},{6,7},{7,8},{8,9},{9,10},{10,1... | collective-permute-start | bytes 786440 | tf_op jit(solution)/shard_map/ppermute | solution.py:33
  266.3 162.9 %collective-permute-start.5 = (bf16[32,2,2048]{2,0,1:T(8,128)(2,1)S(1)}, bf16[32,2,2048]{2,0,1:T(8,128)(2,1)}, u32[]{:S(2)}, u32[]{:S(2)}) collective-permute-start(bf16[32,2,2048]{2,0,1:T(8,128)(2,1)S(1)} %get-tuple-element.103), channel_id=1, source_target_pairs={{1,0},{2,1},{3,2},{4,3},{5,4},{6,5},{7,6},{8,7},{9,8},{10,9},{11,1... | collective-permute-start | bytes 786440 | tf_op jit(solution)/shard_map/ppermute | solution.py:36
  353.6 5.6 %copy-start.33 = (s32[1,96]{1,0:T(1,128)S(1)}, s32[1,96]{1,0:T(1,128)}, u32[]{:S(2)}) copy-start(s32[1,96]{1,0:T(1,128)} %param.22) | copy-start | bytes 1156
  359.3 4.9 %copy-start.31 = (bf16[32,32]{1,0:T(8,128)(2,1)S(1)}, bf16[32,32]{1,0:T(8,128)(2,1)}, u32[]{:S(2)}) copy-start(bf16[32,32]{1,0:T(8,128)(2,1)} %param.25) | copy-start | bytes 6148
Sparse Core Ops, SparseCore 0:
  200.8 146.1 all-reduce.1
where the time goes:
time: 460 us; the launch traced here: 453 us
  local copies, waits for them, and re-layouts  118 us (26%)
  other arithmetic  115 us (25%)
  waiting for transfers between devices  76.9 us (17%)
  blocking collectives  63.5 us (14%)
  matrix products  42.3 us (9%)
  starting transfers between devices  21.2 us (5%)
  between operations  15.8 us (3%)
    psum x1, waiting for transfers between devices, local(): conv_total, mix_total = lax.psum((conv_part, mix_part), ('rep', 'slab'))  76.9 us
    concatenate x24, other arithmetic, shifted_stack(): rolled = jnp.roll(shaped, (-row_off, -col_off), (2, 3))  69.1 us
    psum x1, blocking collectives, local(): conv_total, mix_total = lax.psum((conv_part, mix_part), ('rep', 'slab'))  63.5 us
    reshape x16, local copies, waits for them, and re-layouts, shifted_stack(): pieces.append(rolled.reshape(C, planes, GY * GX))  51.4 us
    scatter-add x4, other arithmetic, over_tiles(): return jax.ops.segment_sum(products, target_ids, num_segments=segments)  34.8 us
    unnamed x87, local copies, waits for them, and re-layouts  18.3 us
    ppermute x4, starting transfers between devices, extended_2(): lax.ppermute(lax.slice_in_dim(block, 0, width, axis=dim), axis, backward)  14.8 us
    dot_general x2, matrix products, deposit_tiles(): jnp.einsum('ctk,tkn->tcn', picked, weights, preferred_element_type=jnp.fl...  13 us
  transfers between devices with their start and end apart: 13, of which 1 were waited for; matrix products, arithmetic and copies ran while one was open for 44% of the time, Pallas kernels for 0%

commit v1 on v0

v1 whole, which is shorter than its diff:
```python
import math

import jax
import jax.numpy as jnp
from jax import lax
from jax.experimental import pallas as pl
from jax.experimental.pallas import tpu as pltpu
from jax.sharding import PartitionSpec as P

C = 32
GY = 32
GX = 64
ZD = 4
A_DEV = 1536
TILES = 96
TILE_A = 64
TILE_C = 512
NB = 32
NAB = 24
CELLS = GY * GX
SLABS = 16
REPS = 8
W_CHUNKS = 6
W_STEP = TILES // W_CHUNKS

PREV_C, LAST_C = 0, 96
PREV_A, LAST_A = 128, 224
ATOM, CELL = 248, 344

F32 = jnp.float32
BF16 = jnp.bfloat16


def at(axis, index):
    return {axis: index}


def kernel(
    idx, feats, cot, w_hbm, conv, mix4, mix_t,
    pot, gfe, gout,
    w, src, acc, snd_dn, snd_up, rcv_lo, rcv_hi, shifted, dside, toep1, toep2, rep1, prod, gw,
    win, cacc, gp, rs1, piece, rs2, fin, ag,
    w_sem, h_send, h_recv, p_send, p_recv, s1, r1, s2, r2, s3, r3, s4, r4,
):
    slab = lax.axis_index("slab")
    rep = lax.axis_index("rep")
    up = lax.rem(slab + 1, SLABS)
    down = lax.rem(slab + SLABS - 1, SLABS)

    loads = []
    for k in range(W_CHUNKS):
        part = pl.ds(k * W_STEP, W_STEP)
        loads.append(pltpu.make_async_copy(w_hbm.at[part], w.at[part], w_sem.at[k]))
        loads[-1].start()

    barrier = pltpu.get_barrier_semaphore()
    for k in range(1, SLABS):
        pl.semaphore_signal(barrier, inc=1, device_id=at("slab", lax.rem(slab + k, SLABS)),
                            device_id_type=pl.DeviceIdType.MESH)
    for k in range(1, REPS):
        pl.semaphore_signal(barrier, inc=1, device_id=at("rep", lax.rem(rep + k, REPS)),
                            device_id_type=pl.DeviceIdType.MESH)

    for a in range(NAB):
        cols = slice(a * TILE_A, (a + 1) * TILE_A)
        src[a, :C] = feats[:, cols]
        src[a, C:] = cot[:, cols]
    acc[0] = jnp.zeros((2 * C, TILE_C), F32)
    cacc[0] = jnp.zeros((2 * C, TILE_A), F32)

    def deposit(t, carry):
        value = jnp.dot(src[idx[ATOM + t]], w[t], preferred_element_type=F32)
        acc[t + 1] = value + acc[idx[PREV_C + t]]
        return carry

    for k in range(W_CHUNKS):
        loads[k].wait()
        lax.fori_loop(k * W_STEP, (k + 1) * W_STEP, deposit, 0)

    for f in range(2):
        rows = slice(f * C, (f + 1) * C)
        for p in range(3):
            for q in range(4):
                snd_dn[f, p, q] = acc[idx[LAST_C + p * 4 + q], rows].astype(BF16)
                snd_up[f, p, q] = acc[idx[LAST_C + (p + 5) * 4 + q], rows].astype(BF16)

    pl.semaphore_wait(barrier, SLABS + REPS - 2)
    halos = []
    for f in range(2):
        for side, (source, target, to) in enumerate(((snd_dn, rcv_hi, down), (snd_up, rcv_lo, up))):
            halos.append(pltpu.make_async_remote_copy(
                src_ref=source.at[f], dst_ref=target.at[f],
                send_sem=h_send.at[f, side], recv_sem=h_recv.at[f, side],
                device_id=at("slab", to), device_id_type=pl.DeviceIdType.MESH))
            halos[-1].start()

    lane32 = lax.broadcasted_iota(jnp.int32, (C, 128), 1) // C

    def banded(toep, flip):
        for dx in range(3):
            for zo in range(4):
                for ct in range(5):
                    tile = jnp.zeros((C, 128), F32)
                    for g in range(4):
                        dy, zi = divmod(ct * 4 + g, 6)
                        if dy < 3 and 0 <= zi - zo < 3:
                            off = 9 * (zi - zo) + 3 * dy + dx
                            off = 26 - off if flip else off
                            tile = jnp.where(lane32 == g, rep1[pl.ds(off * C, C)], tile)
                    rows = slice((dx * 4 + zo) * C, (dx * 4 + zo + 1) * C)
                    width = 128 if ct < 4 else 64
                    toep[rows, ct * 128 : ct * 128 + width] = tile[:, :width].astype(BF16)

    rep1[...] = jnp.dot(conv[...], mix4[...], preferred_element_type=F32)
    banded(toep1, False)

    def turned(off, carry):
        part = conv[pl.ds(pl.multiple_of(off * C, C), C)]
        wide = jnp.concatenate([part] * 4, axis=0)
        rep1[pl.ds(pl.multiple_of(off * C, C), C)] = lax.dot_general(
            mix_t[...], wide, (((1,), (1,)), ((), ())), preferred_element_type=F32)
        return carry

    lax.fori_loop(0, 27, turned, 0)
    banded(toep2, True)

    lane = lax.broadcasted_iota(jnp.int32, (128, 128), 1)
    first_x = lax.rem(lane, GX) == 0
    last_x = lax.rem(lane, GX) == GX - 1

    def next_x(v):
        return jnp.where(last_x[: v.shape[0]], pltpu.roll(v, GX - 1, 1), pltpu.roll(v, 127, 1))

    def prev_x(v):
        return jnp.where(first_x[: v.shape[0]], pltpu.roll(v, 128 - GX + 1, 1), pltpu.roll(v, 1, 1))

    phis = []
    for f in range(2):
        rows = slice(f * C, (f + 1) * C)
        halos[2 * f].wait_recv()
        halos[2 * f + 1].wait_recv()
        for p in range(6):
            got = rcv_lo.at[f, p] if p < 3 else rcv_hi.at[f, p - 3]
            plane = jnp.concatenate(
                [acc[idx[LAST_C + (p + 1) * 4 + q], rows] + got[q].astype(F32) for q in range(4)], axis=1)
            own = slice(p * C, (p + 1) * C)
            shifted[f, 1, own] = plane.astype(BF16)
            shifted[f, 0, own] = pltpu.roll(plane, GX, 1).astype(BF16)
            shifted[f, 2, own] = pltpu.roll(plane, CELLS - GX, 1).astype(BF16)
        toep = toep2 if f else toep1
        for q in range(4):
            cols = slice(q * TILE_C, (q + 1) * TILE_C)
            stack = shifted[f, :, :, cols].reshape(18 * C, TILE_C)
            prod[...] = jnp.dot(toep[...], stack, preferred_element_type=F32)
            for h in range(4):
                part = slice(h * 128, (h + 1) * 128)
                low, mid, high = (prod[d * 128 : (d + 1) * 128, part] for d in range(3))
                phi = (mid + prev_x(low) + next_x(high)).astype(BF16)
                for z in range(ZD):
                    win[f, (z + 2) * 4 + q, :, part] = phi[z * C : (z + 1) * C]
        for side, (start, land, to) in enumerate(((8, 24, down), (16, 0, up))):
            phis.append(pltpu.make_async_remote_copy(
                src_ref=win.at[f, pl.ds(start, 8)], dst_ref=win.at[f, pl.ds(land, 8)],
                send_sem=p_send.at[f, side], recv_sem=p_recv.at[f, side],
                device_id=at("slab", to), device_id_type=pl.DeviceIdType.MESH))
            phis[-1].start()

    for k in range(16):
        cols = slice(k * 128, (k + 1) * 128)
        v = shifted[1, 1, C : 5 * C, cols].astype(F32)
        dside[:128, cols] = next_x(v).astype(BF16)
        dside[128:256, cols] = shifted[1, 1, C : 5 * C, cols]
        dside[256:, cols] = prev_x(v).astype(BF16)
    for dy in range(3):
        gw[dy] = lax.dot_general(dside[...], shifted[0, dy], (((1,), (1,)), ((), ())),
                                 preferred_element_type=F32)
    gp[...] = jnp.zeros_like(gp)
    for off in range(27):
        dz, dy, dx = off // 9, off // 3 % 3, off % 3
        total = None
        for zo in range(ZD):
            rows = slice((dx * 4 + zo) * C, (dx * 4 + zo + 1) * C)
            start = (zo + dz) * C
            part = gw[dy, rows, start : start + C]
            total = part if total is None else total + part
        gp[off // 4, :, off % 4 * C : (off % 4 + 1) * C] = total

    def send(source, target, s_sem, r_sem, axis, to):
        copy = pltpu.make_async_remote_copy(
            src_ref=source, dst_ref=target, send_sem=s_sem, recv_sem=r_sem,
            device_id=at(axis, to), device_id_type=pl.DeviceIdType.MESH)
        copy.start()
        return copy

    sent = []
    now = []
    for k in range(1, REPS):
        to = lax.rem(rep + k, REPS)
        now.append(send(gp.at[to], rs1.at[k], s1.at[k], r1.at[k], "rep", to))
    total = gp[rep]
    for k in range(1, REPS):
        now[k - 1].wait_recv()
        total = total + rs1[k]
    for s in range(SLABS):
        piece[s] = total[2 * s : 2 * s + 2]
    sent += now
    now = []
    for k in range(1, SLABS):
        to = lax.rem(slab + k, SLABS)
        now.append(send(piece.at[to], rs2.at[k], s2.at[k], r2.at[k], "slab", to))
    total = piece[slab]
    for k in range(1, SLABS):
        now[k - 1].wait_recv()
        total = total + rs2[k]
    fin[...] = total
    sent += now
    now = []
    for k in range(1, SLABS):
        to = lax.rem(slab + k, SLABS)
        now.append(send(fin, ag.at[slab], s3.at[k], r3.at[k], "slab", to))
    ag[slab] = fin[...]
    for copy in now:
        copy.wait_recv()
    sent += now
    now = []
    for k in range(1, REPS):
        to = lax.rem(rep + k, REPS)
        now.append(send(ag, gout.at[rep], s4.at[k], r4.at[k], "rep", to))
    gout[rep] = ag[...]

    for copy in phis:
        copy.wait_recv()

    def collect(t, carry):
        cell = idx[CELL + t]
        block = jnp.concatenate([win[0, cell], win[1, cell]], axis=0)
        value = lax.dot_general(block, w[t], (((1,), (1,)), ((), ())), preferred_element_type=F32)
        cacc[t + 1] = value + cacc[idx[PREV_A + t]]
        return carry

    lax.fori_loop(0, TILES, collect, 0)
    for a in range(0, NAB, 2):
        pair = jnp.concatenate([cacc[idx[LAST_A + a]], cacc[idx[LAST_A + a + 1]]], axis=1).astype(BF16)
        cols = slice(a * TILE_A, (a + 2) * TILE_A)
        pot[:, cols] = pair[:C]
        gfe[:, cols] = pair[C:]

    for copy in now:
        copy.wait_recv()
    for copy in sent + now + halos + phis:
        copy.wait_send()


def chains(cells, atoms, live):
    tiles = jnp.arange(TILES, dtype=jnp.int32)
    alive = (tiles < live)[None, :]
    before = tiles[None, :] < tiles[:, None]

    def newest(match):
        return jnp.max(jnp.where(match & alive, tiles[None, :] + 1, 0), axis=1)

    parts = []
    for ids, count in ((cells, NB), (atoms, NAB)):
        parts.append(newest((ids[None, :] == ids[:, None]) & before))
        parts.append(newest(ids[None, :] == jnp.arange(count, dtype=jnp.int32)[:, None]))
    return jnp.concatenate(parts + [atoms, cells])


def local(feats, tile_weight, tile_atom, tile_cell, tile_live, w_mix, conv_w, cotangent):
    idx = chains(tile_cell[0], tile_atom[0], tile_live[0, 0])
    vmem = pl.BlockSpec(memory_space=pltpu.VMEM)
    dma = pltpu.SemaphoreType.DMA
    pot, gfe, total = pl.pallas_call(
        kernel,
        out_shape=(
            jax.ShapeDtypeStruct((C, A_DEV), BF16),
            jax.ShapeDtypeStruct((C, A_DEV), BF16),
            jax.ShapeDtypeStruct((REPS, SLABS, 2, 128), F32),
        ),
        in_specs=[
            pl.BlockSpec(memory_space=pltpu.SMEM), vmem, vmem,
            pl.BlockSpec(memory_space=pl.ANY), vmem, vmem, vmem,
        ],
        out_specs=(vmem, vmem, vmem),
        scratch_shapes=[
            pltpu.VMEM((TILES, TILE_A, TILE_C), BF16),
            pltpu.VMEM((NAB, 2 * C, TILE_A), BF16),
            pltpu.VMEM((TILES + 1, 2 * C, TILE_C), F32),
            pltpu.VMEM((2, 3, 4, C, TILE_C), BF16),
            pltpu.VMEM((2, 3, 4, C, TILE_C), BF16),
            pltpu.VMEM((2, 3, 4, C, TILE_C), BF16),
            pltpu.VMEM((2, 3, 4, C, TILE_C), BF16),
            pltpu.VMEM((2, 3, 6 * C, CELLS), BF16),
            pltpu.VMEM((12 * C, CELLS), BF16),
            pltpu.VMEM((12 * C, 18 * C), BF16),
            pltpu.VMEM((12 * C, 18 * C), BF16),
            pltpu.VMEM((27 * C, 128), F32),
            pltpu.VMEM((12 * C, TILE_C), F32),
            pltpu.VMEM((3, 12 * C, 6 * C), F32),
            pltpu.VMEM((2, NB, C, TILE_C), BF16),
            pltpu.VMEM((TILES + 1, 2 * C, TILE_A), F32),
            pltpu.VMEM((REPS, C, 128), F32),
            pltpu.VMEM((REPS, C, 128), F32),
            pltpu.VMEM((SLABS, 2, 128), F32),
            pltpu.VMEM((SLABS, 2, 128), F32),
            pltpu.VMEM((2, 128), F32),
            pltpu.VMEM((SLABS, 2, 128), F32),
            dma((W_CHUNKS,)), dma((2, 2)), dma((2, 2)), dma((2, 2)), dma((2, 2)),
            dma((REPS,)), dma((REPS,)), dma((SLABS,)), dma((SLABS,)),
            dma((SLABS,)), dma((SLABS,)), dma((REPS,)), dma((REPS,)),
        ],
        compiler_params=pltpu.CompilerParams(
            collective_id=0, has_side_effects=True, vmem_limit_bytes=56 * 2**20,
        ),
    )(
        idx, feats[0], cotangent[0], tile_weight[0], conv_w.reshape(27 * C, C),
        jnp.tile(w_mix, (1, 4)), w_mix.T,
    )
    packed = total.reshape(REPS, C, 4, C)
    moments = jnp.transpose(packed, (0, 2, 1, 3)).reshape(REPS * 4, C, C)[:27]
    exact = lax.Precision.HIGHEST
    conv_total = jnp.einsum("koj,ij->koi", moments, w_mix.astype(F32), precision=exact)
    mix_total = jnp.einsum("kom,koi->mi", conv_w.astype(F32), moments, precision=exact)
    groups = REPS * SLABS
    conv_scale = math.sqrt(groups * ZD * GY * GX)
    mix_scale = math.sqrt(groups * A_DEV)
    return (pot[None], gfe[None], conv_total / conv_scale, mix_total / mix_scale)


def solution(mesh):
    return jax.shard_map(
        local,
        mesh=mesh,
        in_specs=(
            P("rep", None, "slab"),
            P("rep", "slab", None, None),
            P("rep", "slab"),
            P("rep", "slab"),
            P("rep", "slab"),
            P(),
            P(),
            P("rep", None, "slab"),
        ),
        out_specs=(P("rep", None, "slab"), P("rep", None, "slab"), P(), P()),
        check_vma=False,
    )
```

time: 460 us -> 82.5 us (0.18); the launches traced: 453 us -> 82.2 us
  other arithmetic: 115 us -> 2.5 us
  local copies, waits for them, and re-layouts: 118 us -> 9.15 us
  waiting for transfers between devices: 76.9 us -> 0 us
  Pallas kernels: 0 us -> 67.5 us
  blocking collectives: 63.5 us -> 0 us
  matrix products: 42.3 us -> 1.61 us
  starting transfers between devices: 21.2 us -> 0 us
  between operations: 15.8 us -> 1.4 us
    psum x1 -> x0, waiting for transfers between devices: 76.9 us -> none  [local(): conv_total, mix_total = lax.psum((conv_part, mix_part), ('rep', 'slab'))]
    concatenate x29 -> x0, other arithmetic: 72.3 us -> none  [the longest x24 69.1 us: shifted_stack(): rolled = jnp.roll(shaped, (-row_off, -col_off), (2, 3))]
    pallas_call x0 -> x1, Pallas kernels: none -> 67.5 us  [local(): pl.pallas_call(kernel, out_shape=(jax.ShapeDtypeStruct((C, A_DEV), BF16),...]
    reshape x30 -> x1, local copies, waits for them, and re-layouts: 66.7 us -> 1.22 us  [local(): packed = total.reshape(REPS, C, 4, C)]
    psum x1 -> x0, blocking collectives: 63.5 us -> none  [local(): conv_total, mix_total = lax.psum((conv_part, mix_part), ('rep', 'slab'))]
    dot_general x16 -> x2, matrix products: 42.3 us -> 1.61 us  [the longest x1 1.1 us: local(): jnp.einsum('koj,ij->koi', moments, w_mix.astype(F32), precision=exact)]
    scatter-add x8 -> x0, other arithmetic: 37.1 us -> none  [the longest x4 34.8 us: over_tiles(): return jax.ops.segment_sum(products, target_ids, num_segments=segments)]
    ppermute x12 -> x0, starting transfers between devices: 21.1 us -> none  [the longest x4 14.8 us: extended_2(): lax.ppermute(lax.slice_in_dim(block, 0, width, axis=dim), axis, backward)]
  transfers between devices with their start and end apart: 13 -> 0, of which waited for: 1 -> 0; matrix products, arithmetic and copies ran while one was open for 44% -> 0% of each run, Pallas kernels for 0% -> 0%
where the time goes in v1:
time: 82.5 us; the launch traced here: 82.2 us
  Pallas kernels  67.5 us (82%)
  local copies, waits for them, and re-layouts  9.15 us (11%)
  other arithmetic  2.5 us (3%)
  matrix products  1.61 us (2%)
  between operations  1.4 us (2%)
    pallas_call x1, Pallas kernels, local(): pl.pallas_call(kernel, out_shape=(jax.ShapeDtypeStruct((C, A_DEV), BF16),...  67.5 us
    unnamed x8, local copies, waits for them, and re-layouts  5.14 us
    reduce_max x3, other arithmetic, newest(): return jnp.max(jnp.where(match & alive, tiles[None, :] + 1, 0), axis=1)  2.49 us

profile of v1, /device:TPU:1, one launch (start us, length us, event | category | flops | bytes accessed | tf_op | source)
XLA Modules:
  0.0 82.2 jit_solution(12036226772226808868)
XLA Ops:
  0.6 0.0 copy-start.1
  0.6 0.0 copy-start
  1.4 0.8 select_reduce_fusion.3
  2.1 0.8 select_reduce_fusion.2
  2.9 0.9 %select_reduce_fusion = (s32[96]{0:T(128)S(1)}, s32[96]{0:T(128)S(1)}) fusion(s32[96]{0:T(128)} %bitcast.38, s32[96]{0:T(128)S(1)} %iota_add_fusion, pred[96]{0:T(512)(128)(4,1)S(1)} %iota_compare_fusion.3, s32[96]{0:T(128)} %bitcast.41), kind=kLoop, calls=%fused_computation.4 | loop fusion | flops 101184 | bytes 2016 | tf_op jit(solution)/shard_map/reduce_max | solution.py:260
  3.9 1.3 %concatenate.3.idx = s32[440]{0:T(512)} concatenate(s32[96]{0:T(128)S(1)} %get-tuple-element.19, s32[32]{0:T(128)S(1)} %select_reduce_fusion.2, s32[96]{0:T(128)S(1)} %get-tuple-element.18, s32[24]{0:T(128)S(1)} %select_reduce_fusion.3, s32[96]{0:T(128)} %bitcast.39, s32[96]{0:T(128)} %bitcast.42), dimensions={0} | concatenate | bytes 3520 | tf_op jit(solution)/shard_map/concatenate | solution.py:266
  5.2 1.4 %copy.16 = bf16[32,32]{0,1:T(8,128)(2,1)} copy(bf16[32,32]{1,0:T(8,128)(2,1)} %param.13) | data formatting | bytes 4096 | tf_op args[5]
  6.6 0.7 tile.4
  7.3 0.7 tile.10.mix4
  8.0 67.5 %shard_map.111 = (bf16[32,1536]{1,0:T(8,128)(2,1)}, bf16[32,1536]{1,0:T(8,128)(2,1)}, f32[8,16,2,128]{3,2,1,0:T(2,128)}) custom-call(s32[440]{0:T(512)} %concatenate.3.idx, bf16[32,1536]{1,0:T(8,128)(2,1)} %bitcast.34, bf16[32,1536]{1,0:T(8,128)(2,1)} %bitcast.35, bf16[96,64,512]{2,1,0:T(8,128)(2,1)} %bitcast.27, bf16[864,32]{1,0:T(8,128)(2,1)} %bitcast.31, ...), custom_call_target="tpu_custom_call" | custom-call | tf_op jit(solution)/shard_map/pallas_call | solution.py:273
  75.5 1.2 %reshape.33 = f32[8,32,4,32]{3,2,1,0:T(4,128)S(1)} reshape(f32[8,16,2,128]{3,2,1,0:T(2,128)} %get-tuple-element.9) | data formatting | bytes 262144 | tf_op jit(solution)/shard_map/reshape | solution.py:319
  76.7 0.1 copy.17
  76.8 0.0 copy-done
  76.8 0.5 fusion.1
  77.3 0.0 copy-done.1
  77.3 1.1 %convolution_multiply_fusion = f32[27,32,32]{2,1,0:T(8,128)} fusion(f32[32,32,32]{2,1,0:T(8,128)S(1)} %bitcast.29, bf16[32,32]{1,0:T(8,128)(2,1)S(1)} %copy-done.1), kind=kOutput, calls=%fused_computation | convolution fusion | flops 10644480 | bytes 243712 | tf_op jit(solution)/shard_map/koj,ij->koi/dot_general | solution.py:322
  78.4 0.7 copy.19
  79.1 1.5 %copy.24 = bf16[1,32,1536]{2,1,0:T(8,128)(2,1)} copy(bf16[1,32,1536]{2,1,0:T(8,128)(2,1)} %bitcast.33) | data formatting | bytes 196608
  80.6 1.5 %copy.25 = bf16[1,32,1536]{2,1,0:T(8,128)(2,1)} copy(bf16[1,32,1536]{2,1,0:T(8,128)(2,1)} %bitcast.32) | data formatting | bytes 196608
  (2 shorter events, 0.0 us)
Async XLA Ops:
  0.6 76.7 %copy-start.1 = (bf16[32,32]{1,0:T(8,128)(2,1)S(1)}, bf16[32,32]{1,0:T(8,128)(2,1)}, u32[]{:S(2)}) copy-start(bf16[32,32]{1,0:T(8,128)(2,1)} %param.13) | copy-start | bytes 6148
  0.6 76.1 %copy-start = (bf16[27,32,32]{2,1,0:T(8,128)(2,1)S(1)}, bf16[27,32,32]{2,1,0:T(8,128)(2,1)}, u32[]{:S(2)}) copy-start(bf16[27,32,32]{2,1,0:T(8,128)(2,1)} %param.14) | copy-start | bytes 165892

commit v2 on v1

v2 whole, which is shorter than its diff:
```python
import math

import jax
import jax.numpy as jnp
from jax import lax
from jax.experimental import pallas as pl
from jax.experimental.pallas import tpu as pltpu
from jax.sharding import PartitionSpec as P

C = 32
GY = 32
GX = 64
ZD = 4
A_DEV = 1536
TILES = 96
TILE_A = 64
TILE_C = 512
NB = 32
NAB = 24
CELLS = GY * GX
SLABS = 16
REPS = 8
W_CHUNKS = 6
W_STEP = TILES // W_CHUNKS

GROUP = 16
UNROLL = 8
PREV_C, LAST_C, PREV_A, LAST_A, ATOM, CELL = range(6)

F32 = jnp.float32
BF16 = jnp.bfloat16
NT = (((1,), (1,)), ((), ()))
MESH = pl.DeviceIdType.MESH


def kernel(
    feats_hbm, w_hbm, atom_hbm, cell_hbm, live, mix_hbm, conv_hbm, cot_hbm,
    pot, gfe, gout,
    feats, cot, conv, mix, atom_v, cell_v, idx_v, idx,
    w, src, acc, snd_dn, snd_up, rcv_lo, rcv_hi, shifted, dside, toep1, toep2, rep1, prod, gw,
    win, cacc, gp, rs1, rs2, piece, fin,
    in_sem, w_sem, h_send, h_recv, p_send, p_recv, g_send, g_recv,
):
    slab = lax.axis_index("slab")
    rep = lax.axis_index("rep")
    chip, core = slab // 2, lax.rem(slab, 2)
    up = lax.rem(slab + 1, SLABS)
    down = lax.rem(slab + SLABS - 1, SLABS)
    member = rep * 2 + core

    small = []
    pairs = ((cell_hbm, cell_v), (atom_hbm, atom_v), (feats_hbm, feats), (cot_hbm, cot),
             (mix_hbm, mix), (conv_hbm, conv))
    for k, (source, target) in enumerate(pairs):
        small.append(pltpu.make_async_copy(source, target, in_sem.at[k]))
        small[-1].start()
    loads = []
    for k in range(W_CHUNKS):
        part = pl.ds(k * W_STEP, W_STEP)
        loads.append(pltpu.make_async_copy(w_hbm.at[part], w.at[part], w_sem.at[k]))
        loads[-1].start()

    def plane_mate(k):
        other = lax.rem(member + k, GROUP)
        return {"rep": other // 2, "slab": chip * 2 + lax.rem(other, 2)}

    def row_mate(k):
        return {"slab": lax.rem(chip + k, SLABS // 2) * 2 + core}

    mates = [plane_mate(k) for k in range(1, GROUP)] + [row_mate(k) for k in range(1, SLABS // 2)]
    mates += [{"slab": up}, {"slab": down}]
    barrier = pltpu.get_barrier_semaphore()
    for mate in mates:
        pl.semaphore_signal(barrier, inc=1, device_id=mate, device_id_type=MESH)

    small[0].wait()
    small[1].wait()
    lane = lax.broadcasted_iota(jnp.int32, (TILES, TILES), 1)
    sub = lax.broadcasted_iota(jnp.int32, (TILES, TILES), 0)
    alive = sub < live[0, 0]
    number = sub + 1
    for ids, prev, last, copied, limit in (
        (cell_v, PREV_C, LAST_C, CELL, NB - 1), (atom_v, PREV_A, LAST_A, ATOM, NAB - 1)
    ):
        row = jnp.broadcast_to(ids[...], (TILES, TILES))
        column = jnp.sum(jnp.where(lane == sub, row, 0), axis=1, keepdims=True)
        before = jnp.where((column == row) & (sub < lane) & alive, number, 0)
        newest = jnp.where((column == lane) & alive, number, 0)
        idx_v[prev : prev + 1, :TILES] = jnp.clip(jnp.max(before, axis=0, keepdims=True), 0, TILES)
        idx_v[last : last + 1, :TILES] = jnp.clip(jnp.max(newest, axis=0, keepdims=True), 0, TILES)
        idx_v[copied : copied + 1, :TILES] = jnp.clip(ids[...], 0, limit)
    table = pltpu.make_async_copy(idx_v, idx, in_sem.at[6])
    table.start()

    small[2].wait()
    small[3].wait()
    for a in range(NAB):
        cols = slice(a * TILE_A, (a + 1) * TILE_A)
        src[a, :C] = feats[:, cols]
        src[a, C:] = cot[:, cols]
    acc[0] = jnp.zeros((2 * C, TILE_C), F32)
    cacc[0] = jnp.zeros((2 * C, TILE_A), F32)
    table.wait()

    def deposit(i, carry):
        first = i * UNROLL
        values = [jnp.dot(src[idx[ATOM, first + u]], w[first + u], preferred_element_type=F32) for u in range(UNROLL)]
        for u in range(UNROLL):
            acc[first + u + 1] = values[u] + acc[idx[PREV_C, first + u]]
        return carry

    steps = W_STEP // UNROLL
    for k in range(W_CHUNKS):
        loads[k].wait()
        lax.fori_loop(k * steps, (k + 1) * steps, deposit, 0)

    pl.semaphore_wait(barrier, len(mates))
    halos = []
    groups = []
    sides = ((snd_dn, rcv_hi, down, 0), (snd_up, rcv_lo, up, 5))
    for stage, (f, wanted) in enumerate(((0, ((0, 1, 2), (2, 1, 0))), (1, ((0, 1), (2, 1))), (1, ((2,), (0,))))):
        rows = slice(f * C, (f + 1) * C)
        for j in range(len(wanted[0])):
            for side, (source, target, to, base) in enumerate(sides):
                k = wanted[side][j]
                for q in range(4):
                    source[f, k, q] = acc[idx[LAST_C, (base + k) * 4 + q], rows].astype(BF16)
                copy = pltpu.make_async_remote_copy(
                    src_ref=source.at[f, k], dst_ref=target.at[f, k],
                    send_sem=h_send.at[stage, side], recv_sem=h_recv.at[stage, side],
                    device_id={"slab": to}, device_id_type=MESH)
                copy.start()
        for side, (source, target, to, base) in enumerate(sides):
            first, count = min(wanted[side]), len(wanted[side])
            halos.append(pltpu.make_async_remote_copy(
                src_ref=source.at[f, pl.ds(first, count)], dst_ref=target.at[f, pl.ds(first, count)],
                send_sem=h_send.at[stage, side], recv_sem=h_recv.at[stage, side],
                device_id={"slab": to}, device_id_type=MESH))

    small[4].wait()
    small[5].wait()
    lane32 = lax.broadcasted_iota(jnp.int32, (C, 128), 1) // C

    def banded(toep, flip):
        for dx in range(3):
            for zo in range(4):
                for ct in range(5):
                    tile = jnp.zeros((C, 128), F32)
                    for g in range(4):
                        dy, zi = divmod(ct * 4 + g, 6)
                        if dy < 3 and 0 <= zi - zo < 3:
                            off = 9 * (zi - zo) + 3 * dy + dx
                            off = 26 - off if flip else off
                            tile = jnp.where(lane32 == g, rep1[pl.ds(off * C, C)], tile)
                    rows = slice((dx * 4 + zo) * C, (dx * 4 + zo + 1) * C)
                    width = 128 if ct < 4 else 64
                    toep[rows, ct * 128 : ct * 128 + width] = tile[:, :width].astype(BF16)

    mixing = mix[...]
    rep1[...] = jnp.dot(
        conv[...].reshape(27 * C, C), jnp.concatenate([mixing] * 4, axis=1), preferred_element_type=F32)
    banded(toep1, False)
    mix_t = mixing.astype(F32).T.astype(BF16)

    def turned(off, carry):
        wide = jnp.concatenate([conv[off]] * 4, axis=0)
        rep1[pl.ds(pl.multiple_of(off * C, C), C)] = lax.dot_general(mix_t, wide, NT, preferred_element_type=F32)
        return carry

    lax.fori_loop(0, 27, turned, 0)
    banded(toep2, True)

    spot = lax.broadcasted_iota(jnp.int32, (128, 128), 1)
    first_x = lax.rem(spot, GX) == 0
    last_x = lax.rem(spot, GX) == GX - 1

    def next_x(v):
        return jnp.where(last_x, pltpu.roll(v, GX - 1, 1), pltpu.roll(v, 127, 1))

    def prev_x(v):
        return jnp.where(first_x, pltpu.roll(v, 128 - GX + 1, 1), pltpu.roll(v, 1, 1))

    def stack(f, p):
        got = rcv_lo.at[f, p] if p < 3 else rcv_hi.at[f, p - 3]
        rows = slice(f * C, (f + 1) * C)
        plane = jnp.concatenate(
            [acc[idx[LAST_C, (p + 1) * 4 + q], rows] + got[q].astype(F32) for q in range(4)], axis=1)
        own = slice(p * C, (p + 1) * C)
        shifted[f, 1, own] = plane.astype(BF16)
        shifted[f, 0, own] = pltpu.roll(plane, GX, 1).astype(BF16)
        shifted[f, 2, own] = pltpu.roll(plane, CELLS - GX, 1).astype(BF16)

    phis = []

    def convolve(f):
        toep = toep2 if f else toep1
        for q in range(4):
            cols = slice(q * TILE_C, (q + 1) * TILE_C)
            stacked = shifted[f, :, :, cols].reshape(18 * C, TILE_C)
            prod[...] = jnp.dot(toep[...], stacked, preferred_element_type=F32)
            for h in range(4):
                part = slice(h * 128, (h + 1) * 128)
                low, mid, high = (prod[d * 128 : (d + 1) * 128, part] for d in range(3))
                phi = (mid + prev_x(low) + next_x(high)).astype(BF16)
                for z in range(ZD):
                    win[f, (z + 2) * 4 + q, :, part] = phi[z * C : (z + 1) * C]
        for side, (start, land, to) in enumerate(((8, 24, down), (16, 0, up))):
            phis.append(pltpu.make_async_remote_copy(
                src_ref=win.at[f, pl.ds(start, 8)], dst_ref=win.at[f, pl.ds(land, 8)],
                send_sem=p_send.at[f, side], recv_sem=p_recv.at[f, side],
                device_id={"slab": to}, device_id_type=MESH))
            phis[-1].start()

    halos[0].wait_recv()
    halos[1].wait_recv()
    for p in range(6):
        stack(0, p)
    convolve(0)

    halos[2].wait_recv()
    halos[3].wait_recv()
    for p in range(1, 5):
        stack(1, p)
    for k in range(16):
        cols = slice(k * 128, (k + 1) * 128)
        v = shifted[1, 1, C : 5 * C, cols].astype(F32)
        dside[:128, cols] = next_x(v).astype(BF16)
        dside[128:256, cols] = shifted[1, 1, C : 5 * C, cols]
        dside[256:, cols] = prev_x(v).astype(BF16)
    for dy in range(3):
        gw[dy] = lax.dot_general(dside[...], shifted[0, dy], NT, preferred_element_type=F32)
    for off in range(27):
        dz, dy, dx = off // 9, off // 3 % 3, off % 3
        total = None
        for zo in range(ZD):
            rows = slice((dx * 4 + zo) * C, (dx * 4 + zo + 1) * C)
            start = (zo + dz) * C
            part = gw[dy, rows, start : start + C]
            total = part if total is None else total + part
        block, cols = off // 4, slice(off % 4 * C, (off % 4 + 1) * C)
        gp[2 * block, :, cols] = total[: C // 2]
        gp[2 * block + 1, :, cols] = total[C // 2 :]
    gp[13, :, 3 * C :] = jnp.zeros((C // 2, C), F32)
    gp[12, :, 3 * C :] = jnp.zeros((C // 2, C), F32)
    gp[14:] = jnp.zeros((2, C // 2, 128), F32)

    def give(source, target, phase, mate):
        pltpu.make_async_remote_copy(
            src_ref=source, dst_ref=target, send_sem=g_send.at[phase], recv_sem=g_recv.at[phase],
            device_id=mate, device_id_type=MESH).start()

    def all_of(buffer, count, phase):
        part = buffer.at[pl.ds(0, count)]
        return pltpu.make_async_remote_copy(
            src_ref=part, dst_ref=part, send_sem=g_send.at[phase], recv_sem=g_recv.at[phase],
            device_id=plane_mate(1), device_id_type=MESH)

    for k in range(1, GROUP):
        give(gp.at[lax.rem(member + k, GROUP)], rs1.at[k], 0, plane_mate(k))
    rs1[0] = gp[member]

    halos[4].wait_recv()
    halos[5].wait_recv()
    stack(1, 0)
    stack(1, 5)
    convolve(1)

    all_of(rs1, GROUP - 1, 0).wait_recv()
    piece[...] = jnp.sum(rs1[...], axis=0)
    for k in range(1, SLABS // 2):
        give(piece, rs2.at[chip], 1, row_mate(k))
    rs2[chip] = piece[...]

    for copy in phis:
        copy.wait_recv()

    def collect(i, carry):
        first = i * UNROLL
        values = []
        for u in range(UNROLL):
            cell = idx[CELL, first + u]
            block = jnp.concatenate([win[0, cell], win[1, cell]], axis=0)
            values.append(lax.dot_general(block, w[first + u], NT, preferred_element_type=F32))
        for u in range(UNROLL):
            cacc[first + u + 1] = values[u] + cacc[idx[PREV_A, first + u]]
        return carry

    lax.fori_loop(0, 4, collect, 0)

    all_of(rs2, SLABS // 2 - 1, 1).wait_recv()
    fin[...] = jnp.sum(rs2[...], axis=0)
    for k in range(1, GROUP):
        give(fin, gout.at[member], 2, plane_mate(k))
    gout[member] = fin[...]

    lax.fori_loop(4, TILES // UNROLL, collect, 0)
    for a in range(0, NAB, 2):
        pair = jnp.concatenate([cacc[idx[LAST_A, a]], cacc[idx[LAST_A, a + 1]]], axis=1).astype(BF16)
        cols = slice(a * TILE_A, (a + 2) * TILE_A)
        pot[:, cols] = pair[:C]
        gfe[:, cols] = pair[C:]

    all_of(gout, GROUP - 1, 2).wait_recv()
    all_of(gout, GROUP - 1, 2).wait_send()
    all_of(rs2, SLABS // 2 - 1, 1).wait_send()
    all_of(rs1, GROUP - 1, 0).wait_send()
    for copy in halos + phis:
        copy.wait_send()


def finish(pot_in, gfe_in, moments, mix, conv, pot, gfe, gconv, gmix, flat):
    pot[...] = pot_in[...]
    gfe[...] = gfe_in[...]
    for off in range(27):
        block, cols = off // 4, slice(off % 4 * C, (off % 4 + 1) * C)
        flat[off * C : off * C + C // 2] = moments[2 * block, :, cols]
        flat[off * C + C // 2 : (off + 1) * C] = moments[2 * block + 1, :, cols]
    value = flat[...]
    high = value.astype(BF16)
    low = (value - high.astype(F32)).astype(BF16)
    mixing = mix[...]
    turned = conv[...].reshape(27 * C, C).astype(F32).T.astype(BF16)
    devices = REPS * SLABS
    conv_scale = 1.0 / math.sqrt(devices * ZD * GY * GX)
    mix_scale = 1.0 / math.sqrt(devices * A_DEV)
    product = (lax.dot_general(high, mixing, NT, preferred_element_type=F32)
               + lax.dot_general(low, mixing, NT, preferred_element_type=F32))
    gconv[...] = (product * conv_scale).reshape(27, C, C)
    gmix[...] = (jnp.dot(turned, high, preferred_element_type=F32)
                 + jnp.dot(turned, low, preferred_element_type=F32)) * mix_scale


def local(feats, tile_weight, tile_atom, tile_cell, tile_live, w_mix, conv_w, cotangent):
    vmem = pl.BlockSpec(memory_space=pltpu.VMEM)
    hbm = pl.BlockSpec(memory_space=pl.ANY)
    dma = pltpu.SemaphoreType.DMA
    field = jax.ShapeDtypeStruct((C, A_DEV), BF16)
    pot, gfe, total = pl.pallas_call(
        kernel,
        out_shape=(field, field, jax.ShapeDtypeStruct((GROUP, C // 2, 128), F32)),
        in_specs=[hbm] * 4 + [pl.BlockSpec(memory_space=pltpu.SMEM)] + [hbm] * 3,
        out_specs=(vmem, vmem, vmem),
        scratch_shapes=[
            pltpu.VMEM((C, A_DEV), BF16),
            pltpu.VMEM((C, A_DEV), BF16),
            pltpu.VMEM((27, C, C), BF16),
            pltpu.VMEM((C, C), BF16),
            pltpu.VMEM((1, TILES), jnp.int32),
            pltpu.VMEM((1, TILES), jnp.int32),
            pltpu.VMEM((8, 128), jnp.int32),
            pltpu.SMEM((8, 128), jnp.int32),
            pltpu.VMEM((TILES, TILE_A, TILE_C), BF16),
            pltpu.VMEM((NAB, 2 * C, TILE_A), BF16),
            pltpu.VMEM((TILES + 1, 2 * C, TILE_C), F32),
            pltpu.VMEM((2, 3, 4, C, TILE_C), BF16),
            pltpu.VMEM((2, 3, 4, C, TILE_C), BF16),
            pltpu.VMEM((2, 3, 4, C, TILE_C), BF16),
            pltpu.VMEM((2, 3, 4, C, TILE_C), BF16),
            pltpu.VMEM((2, 3, 6 * C, CELLS), BF16),
            pltpu.VMEM((12 * C, CELLS), BF16),
            pltpu.VMEM((12 * C, 18 * C), BF16),
            pltpu.VMEM((12 * C, 18 * C), BF16),
            pltpu.VMEM((27 * C, 128), F32),
            pltpu.VMEM((12 * C, TILE_C), F32),
            pltpu.VMEM((3, 12 * C, 6 * C), F32),
            pltpu.VMEM((2, NB, C, TILE_C), BF16),
            pltpu.VMEM((TILES + 1, 2 * C, TILE_A), F32),
            pltpu.VMEM((GROUP, C // 2, 128), F32),
            pltpu.VMEM((GROUP, C // 2, 128), F32),
            pltpu.VMEM((SLABS // 2, C // 2, 128), F32),
            pltpu.VMEM((C // 2, 128), F32),
            pltpu.VMEM((C // 2, 128), F32),
            dma((7,)), dma((W_CHUNKS,)), dma((3, 2)), dma((3, 2)), dma((2, 2)), dma((2, 2)), dma((3,)), dma((3,)),
        ],
        compiler_params=pltpu.CompilerParams(
            collective_id=0, has_side_effects=True, vmem_limit_bytes=56 * 2**20,
        ),
    )(feats[0], tile_weight[0], tile_atom, tile_cell, tile_live, w_mix, conv_w, cotangent[0])
    pot, gfe, gconv, gmix = pl.pallas_call(
        finish,
        out_shape=(field, field, jax.ShapeDtypeStruct((27, C, C), F32), jax.ShapeDtypeStruct((C, C), F32)),
        in_specs=[vmem] * 5,
        out_specs=(vmem,) * 4,
        scratch_shapes=[pltpu.VMEM((27 * C, C), F32)],
        compiler_params=pltpu.CompilerParams(vmem_limit_bytes=32 * 2**20),
    )(pot, gfe, total, w_mix, conv_w)
    return pot[None], gfe[None], gconv, gmix


def solution(mesh):
    return jax.shard_map(
        local,
        mesh=mesh,
        in_specs=(
            P("rep", None, "slab"),
            P("rep", "slab", None, None),
            P("rep", "slab"),
            P("rep", "slab"),
            P("rep", "slab"),
            P(),
            P(),
            P("rep", None, "slab"),
        ),
        out_specs=(P("rep", None, "slab"), P("rep", None, "slab"), P(), P()),
        check_vma=False,
    )
```

time: 82.5 us -> 43.8 us (0.53)
  Pallas kernels: 67.5 us -> 39.5 us
  local copies, waits for them, and re-layouts: 9.15 us -> 2.69 us
  other arithmetic: 2.5 us -> 0 us
  matrix products: 1.61 us -> 0 us
    pallas_call x1 -> x2, Pallas kernels: 67.5 us -> 39.5 us  [the longest x1 38.3 us: local(): pl.pallas_call(kernel, out_shape=(field, field, jax.ShapeDtypeStruct((GRO...]
    reduce_max x3 -> x0, other arithmetic: 2.49 us -> none  [newest(): return jnp.max(jnp.where(match & alive, tiles[None, :] + 1, 0), axis=1)]
    unnamed x8 -> x10, local copies, waits for them, and re-layouts: 5.14 us -> 2.69 us
    dot_general x2 -> x0, matrix products: 1.61 us -> none  [the longest x1 1.1 us: local(): jnp.einsum('koj,ij->koi', moments, w_mix.astype(F32), precision=exact)]
    another operation x2 -> x0, local copies, waits for them, and re-layouts: 1.4 us -> none  [local(): jnp.tile(w_mix, (1, 4))]
    concatenate x1 -> x0, local copies, waits for them, and re-layouts: 1.34 us -> none  [chains(): return jnp.concatenate(parts + [atoms, cells])]
    reshape x1 -> x0, local copies, waits for them, and re-layouts: 1.22 us -> none  [local(): packed = total.reshape(REPS, C, 4, C)]
where the time goes in v2:
time: 43.8 us; the launch traced here: 43.6 us
  Pallas kernels  39.5 us (90%)
  local copies, waits for them, and re-layouts  2.69 us (6%)
  between operations  1.37 us (3%)
    pallas_call x1, Pallas kernels, local(): pl.pallas_call(kernel, out_shape=(field, field, jax.ShapeDtypeStruct((GRO...  38.3 us
    unnamed x10, local copies, waits for them, and re-layouts  2.69 us
    pallas_call x1, Pallas kernels, local(): pl.pallas_call(finish, out_shape=(field, field, jax.ShapeDtypeStruct((27,...  1.19 us

profile of v2, /device:TPU:1, one launch (start us, length us, event | category | flops | bytes accessed | tf_op | source)
XLA Modules:
  0.0 43.6 jit_solution(4682832356432508469)
XLA Ops:
  0.6 0.0 copy-start
  0.6 0.0 copy-start.4
  1.3 38.3 %shard_map.111 = (bf16[32,1536]{1,0:T(8,128)(2,1)}, bf16[32,1536]{1,0:T(8,128)(2,1)}, f32[16,16,128]{2,1,0:T(8,128)}) custom-call(bf16[32,1536]{1,0:T(8,128)(2,1)} %bitcast.6, bf16[96,64,512]{2,1,0:T(8,128)(2,1)} %bitcast.5, s32[1,96]{1,0:T(1,128)} %atom_hbm.1, s32[1,96]{1,0:T(1,128)} %cell_hbm.1, s32[1,1]{1,0:T(1,128)S(6)} %copy.12.live, ...), custom_call_target="tpu_custom_call" | custom-call | tf_op jit(solution)/shard_map/pallas_call | solution.py:338
  39.7 0.0 copy-done
  39.7 0.0 copy-done.4
  39.7 0.0 copy-start.1
  39.7 0.9 %copy-done.1 = f32[16,16,128]{2,1,0:T(8,128)S(1)} copy-done((f32[16,16,128]{2,1,0:T(8,128)S(1)}, f32[16,16,128]{2,1,0:T(8,128)}, u32[]{:S(2)}) %copy-start.1) | copy-done | bytes 131096
  40.6 0.0 copy-start.2
  40.6 0.9 %copy-done.2 = bf16[32,1536]{1,0:T(8,128)(2,1)S(1)} copy-done((bf16[32,1536]{1,0:T(8,128)(2,1)S(1)}, bf16[32,1536]{1,0:T(8,128)(2,1)}, u32[]{:S(2)}) %copy-start.2) | copy-done | bytes 98328
  41.5 0.0 copy-start.3
  41.5 0.9 %copy-done.3 = bf16[32,1536]{1,0:T(8,128)(2,1)S(1)} copy-done((bf16[32,1536]{1,0:T(8,128)(2,1)S(1)}, bf16[32,1536]{1,0:T(8,128)(2,1)}, u32[]{:S(2)}) %copy-start.3) | copy-done | bytes 98328
  42.4 1.2 %shard_map.112 = (bf16[32,1536]{1,0:T(8,128)(2,1)}, bf16[32,1536]{1,0:T(8,128)(2,1)}, f32[27,32,32]{2,1,0:T(8,128)}, f32[32,32]{1,0:T(8,128)}) custom-call(bf16[32,1536]{1,0:T(8,128)(2,1)S(1)} %copy-done.2, bf16[32,1536]{1,0:T(8,128)(2,1)S(1)} %copy-done.3, f32[16,16,128]{2,1,0:T(8,128)S(1)} %copy-done.1, bf16[32,32]{1,0:T(8,128)(2,1)S(1)} %copy-done.4, ...), custom_call_target="tpu_custom_call" | custom-call | tf_op jit(solution)/shard_map/pallas_call | solution.py:379
Async XLA Ops:
  0.6 39.0 %copy-start = (bf16[27,32,32]{2,1,0:T(8,128)(2,1)S(1)}, bf16[27,32,32]{2,1,0:T(8,128)(2,1)}, u32[]{:S(2)}) copy-start(bf16[27,32,32]{2,1,0:T(8,128)(2,1)} %conv.1) | copy-start | bytes 165892
  0.6 39.0 %copy-start.4 = (bf16[32,32]{1,0:T(8,128)(2,1)S(1)}, bf16[32,32]{1,0:T(8,128)(2,1)}, u32[]{:S(2)}) copy-start(bf16[32,32]{1,0:T(8,128)(2,1)} %mix.1) | copy-start | bytes 6148
  39.7 0.9 %copy-start.1 = (f32[16,16,128]{2,1,0:T(8,128)S(1)}, f32[16,16,128]{2,1,0:T(8,128)}, u32[]{:S(2)}) copy-start(f32[16,16,128]{2,1,0:T(8,128)} %get-tuple-element.13.moments) | copy-start | bytes 393220
  40.6 0.9 %copy-start.2 = (bf16[32,1536]{1,0:T(8,128)(2,1)S(1)}, bf16[32,1536]{1,0:T(8,128)(2,1)}, u32[]{:S(2)}) copy-start(bf16[32,1536]{1,0:T(8,128)(2,1)} %get-tuple-element.11.pot_in) | copy-start | bytes 294916
  41.5 0.9 %copy-start.3 = (bf16[32,1536]{1,0:T(8,128)(2,1)S(1)}, bf16[32,1536]{1,0:T(8,128)(2,1)}, u32[]{:S(2)}) copy-start(bf16[32,1536]{1,0:T(8,128)(2,1)} %get-tuple-element.12.gfe_in) | copy-start | bytes 294916

commit v3 on v2

--- a/solution.py
+++ b/solution.py
@@ -36,10 +36,10 @@
 def kernel(
     feats_hbm, w_hbm, atom_hbm, cell_hbm, live, mix_hbm, conv_hbm, cot_hbm,
     pot, gfe, gout,
-    feats, cot, conv, mix, atom_v, cell_v, idx_v, idx,
+    pot_v, gfe_v, feats, cot, conv, mix, atom_v, cell_v, idx_v, idx,
     w, src, acc, snd_dn, snd_up, rcv_lo, rcv_hi, shifted, dside, toep1, toep2, rep1, prod, gw,
-    win, cacc, gp, rs1, rs2, piece, fin,
-    in_sem, w_sem, h_send, h_recv, p_send, p_recv, g_send, g_recv,
+    win0, win1, cacc, gp, rs1, rs2, piece, fin,
+    in_sem, out_sem, w_sem, h_send, h_recv, p_send, p_recv, g_send, g_recv,
 ):
     slab = lax.axis_index("slab")
     rep = lax.axis_index("rep")
@@ -49,8 +49,8 @@
     member = rep * 2 + core
 
     small = []
-    pairs = ((cell_hbm, cell_v), (atom_hbm, atom_v), (feats_hbm, feats), (cot_hbm, cot),
-             (mix_hbm, mix), (conv_hbm, conv))
+    pairs = ((cell_hbm, cell_v), (atom_hbm, atom_v), (feats_hbm, feats), (mix_hbm, mix),
+             (conv_hbm, conv), (cot_hbm, cot))
     for k, (source, target) in enumerate(pairs):
         small.append(pltpu.make_async_copy(source, target, in_sem.at[k]))
         small[-1].start()
@@ -92,39 +92,40 @@
     table = pltpu.make_async_copy(idx_v, idx, in_sem.at[6])
     table.start()
 
+    def fill(f, values):
+        for a in range(NAB):
+            src[f, a] = values[:, a * TILE_A : (a + 1) * TILE_A]
+        acc[f, 0] = jnp.zeros((C, TILE_C), F32)
+        cacc[f, 0] = jnp.zeros((C, TILE_A), F32)
+
     small[2].wait()
-    small[3].wait()
-    for a in range(NAB):
-        cols = slice(a * TILE_A, (a + 1) * TILE_A)
-        src[a, :C] = feats[:, cols]
-        src[a, C:] = cot[:, cols]
-    acc[0] = jnp.zeros((2 * C, TILE_C), F32)
-    cacc[0] = jnp.zeros((2 * C, TILE_A), F32)
+    fill(0, feats)
     table.wait()
 
-    def deposit(i, carry):
-        first = i * UNROLL
-        values = [jnp.dot(src[idx[ATOM, first + u]], w[first + u], preferred_element_type=F32) for u in range(UNROLL)]
-        for u in range(UNROLL):
-            acc[first + u + 1] = values[u] + acc[idx[PREV_C, first + u]]
-        return carry
-
-    steps = W_STEP // UNROLL
+    def deposit(f, start, stop):
+        def body(i, carry):
+            first = i * UNROLL
+            values = [jnp.dot(src[f, idx[ATOM, first + u]], w[first + u], preferred_element_type=F32)
+                      for u in range(UNROLL)]
+            for u in range(UNROLL):
+                acc[f, first + u + 1] = values[u] + acc[f, idx[PREV_C, first + u]]
+            return carry
+
+        lax.fori_loop(start // UNROLL, stop // UNROLL, body, 0)
+
     for k in range(W_CHUNKS):
         loads[k].wait()
-        lax.fori_loop(k * steps, (k + 1) * steps, deposit, 0)
-
-    pl.semaphore_wait(barrier, len(mates))
+        deposit(0, k * W_STEP, (k + 1) * W_STEP)
+
     halos = []
-    groups = []
     sides = ((snd_dn, rcv_hi, down, 0), (snd_up, rcv_lo, up, 5))
-    for stage, (f, wanted) in enumerate(((0, ((0, 1, 2), (2, 1, 0))), (1, ((0, 1), (2, 1))), (1, ((2,), (0,))))):
-        rows = slice(f * C, (f + 1) * C)
+
+    def exchange(stage, f, wanted):
         for j in range(len(wanted[0])):
             for side, (source, target, to, base) in enumerate(sides):
                 k = wanted[side][j]
                 for q in range(4):
-                    source[f, k, q] = acc[idx[LAST_C, (base + k) * 4 + q], rows].astype(BF16)
+                    source[f, k, q] = acc[f, idx[LAST_C, (base + k) * 4 + q]].astype(BF16)
                 copy = pltpu.make_async_remote_copy(
                     src_ref=source.at[f, k], dst_ref=target.at[f, k],
                     send_sem=h_send.at[stage, side], recv_sem=h_recv.at[stage, side],
@@ -137,8 +138,16 @@
                 send_sem=h_send.at[stage, side], recv_sem=h_recv.at[stage, side],
                 device_id={"slab": to}, device_id_type=MESH))
 
+    pl.semaphore_wait(barrier, len(mates))
+    exchange(0, 0, ((0, 1, 2), (2, 1, 0)))
+    small[5].wait()
+    fill(1, cot)
+    deposit(1, 0, TILES)
+    exchange(1, 1, ((0, 1), (2, 1)))
+    exchange(2, 1, ((2,), (0,)))
+
+    small[3].wait()
     small[4].wait()
-    small[5].wait()
     lane32 = lax.broadcasted_iota(jnp.int32, (C, 128), 1) // C
 
     def banded(toep, flip):
@@ -162,12 +171,9 @@
     banded(toep1, False)
     mix_t = mixing.astype(F32).T.astype(BF16)
 
-    def turned(off, carry):
+    for off in range(27):
         wide = jnp.concatenate([conv[off]] * 4, axis=0)
-        rep1[pl.ds(pl.multiple_of(off * C, C), C)] = lax.dot_general(mix_t, wide, NT, preferred_element_type=F32)
-        return carry
-
-    lax.fori_loop(0, 27, turned, 0)
+        rep1[off * C : (off + 1) * C] = lax.dot_general(mix_t, wide, NT, preferred_element_type=F32)
     banded(toep2, True)
 
     spot = lax.broadcasted_iota(jnp.int32, (128, 128), 1)
@@ -182,15 +188,15 @@
 
     def stack(f, p):
         got = rcv_lo.at[f, p] if p < 3 else rcv_hi.at[f, p - 3]
-        rows = slice(f * C, (f + 1) * C)
         plane = jnp.concatenate(
-            [acc[idx[LAST_C, (p + 1) * 4 + q], rows] + got[q].astype(F32) for q in range(4)], axis=1)
+            [acc[f, idx[LAST_C, (p + 1) * 4 + q]] + got[q].astype(F32) for q in range(4)], axis=1)
         own = slice(p * C, (p + 1) * C)
         shifted[f, 1, own] = plane.astype(BF16)
         shifted[f, 0, own] = pltpu.roll(plane, GX, 1).astype(BF16)
         shifted[f, 2, own] = pltpu.roll(plane, CELLS - GX, 1).astype(BF16)
 
     phis = []
+    win = (win0, win1)
 
     def convolve(f):
         toep = toep2 if f else toep1
@@ -203,10 +209,10 @@
                 low, mid, high = (prod[d * 128 : (d + 1) * 128, part] for d in range(3))
                 phi = (mid + prev_x(low) + next_x(high)).astype(BF16)
                 for z in range(ZD):
-                    win[f, (z + 2) * 4 + q, :, part] = phi[z * C : (z + 1) * C]
+                    win[f][(z + 2) * 4 + q, :, part] = phi[z * C : (z + 1) * C]
         for side, (start, land, to) in enumerate(((8, 24, down), (16, 0, up))):
             phis.append(pltpu.make_async_remote_copy(
-                src_ref=win.at[f, pl.ds(start, 8)], dst_ref=win.at[f, pl.ds(land, 8)],
+                src_ref=win[f].at[pl.ds(start, 8)], dst_ref=win[f].at[pl.ds(land, 8)],
                 send_sem=p_send.at[f, side], recv_sem=p_recv.at[f, side],
                 device_id={"slab": to}, device_id_type=MESH))
             phis[-1].start()
@@ -271,46 +277,56 @@
         give(piece, rs2.at[chip], 1, row_mate(k))
     rs2[chip] = piece[...]
 
-    for copy in phis:
-        copy.wait_recv()
-
-    def collect(i, carry):
-        first = i * UNROLL
-        values = []
-        for u in range(UNROLL):
-            cell = idx[CELL, first + u]
-            block = jnp.concatenate([win[0, cell], win[1, cell]], axis=0)
-            values.append(lax.dot_general(block, w[first + u], NT, preferred_element_type=F32))
-        for u in range(UNROLL):
-            cacc[first + u + 1] = values[u] + cacc[idx[PREV_A, first + u]]
-        return carry
-
-    lax.fori_loop(0, 4, collect, 0)
+    def collect(f):
+        def body(i, carry):
+            first = i * UNROLL
+            values = [lax.dot_general(win[f][idx[CELL, first + u]], w[first + u], NT, preferred_element_type=F32)
+                      for u in range(UNROLL)]
+            for u in range(UNROLL):
+                cacc[f, first + u + 1] = values[u] + cacc[f, idx[PREV_A, first + u]]
+            return carry
+
+        lax.fori_loop(0, TILES // UNROLL, body, 0)
+        out_v, out = (gfe_v, gfe) if f else (pot_v, pot)
+        for a in range(0, NAB, 2):
+            pair = jnp.concatenate([cacc[f, idx[LAST_A, a]], cacc[f, idx[LAST_A, a + 1]]], axis=1)
+            out_v[:, a * TILE_A : (a + 2) * TILE_A] = pair.astype(BF16)
+        copy = pltpu.make_async_copy(out_v, out, out_sem.at[f])
+        copy.start()
+        return copy
+
+    phis[0].wait_recv()
+    phis[1].wait_recv()
+    outs = [collect(0)]
 
     all_of(rs2, SLABS // 2 - 1, 1).wait_recv()
     fin[...] = jnp.sum(rs2[...], axis=0)
     for k in range(1, GROUP):
         give(fin, gout.at[member], 2, plane_mate(k))
-    gout[member] = fin[...]
-
-    lax.fori_loop(4, TILES // UNROLL, collect, 0)
-    for a in range(0, NAB, 2):
-        pair = jnp.concatenate([cacc[idx[LAST_A, a]], cacc[idx[LAST_A, a + 1]]], axis=1).astype(BF16)
-        cols = slice(a * TILE_A, (a + 2) * TILE_A)
-        pot[:, cols] = pair[:C]
-        gfe[:, cols] = pair[C:]
-
-    all_of(gout, GROUP - 1, 2).wait_recv()
-    all_of(gout, GROUP - 1, 2).wait_send()
+    outs.append(pltpu.make_async_copy(fin, gout.at[member], out_sem.at[2]))
+    outs[-1].start()
+
+    phis[2].wait_recv()
+    phis[3].wait_recv()
+    outs.append(collect(1))
+
+    all_of(rs1, GROUP - 1, 0).wait_send()
     all_of(rs2, SLABS // 2 - 1, 1).wait_send()
-    all_of(rs1, GROUP - 1, 0).wait_send()
     for copy in halos + phis:
         copy.wait_send()
-
-
-def finish(pot_in, gfe_in, moments, mix, conv, pot, gfe, gconv, gmix, flat):
-    pot[...] = pot_in[...]
-    gfe[...] = gfe_in[...]
+    all_of(rs1, GROUP - 1, 2).wait_send()
+    all_of(rs1, GROUP - 1, 2).wait_recv()
+    for copy in outs:
+        copy.wait()
+
+
+def finish(pot_in, gfe_in, moments_hbm, mix_hbm, conv_hbm, pot, gfe, gconv, gmix, moments, mix, conv, flat, sem):
+    pairs = ((moments_hbm, moments), (mix_hbm, mix), (conv_hbm, conv), (pot_in, pot), (gfe_in, gfe))
+    copies = [pltpu.make_async_copy(source, target, sem.at[k]) for k, (source, target) in enumerate(pairs)]
+    for copy in copies:
+        copy.start()
+    for copy in copies[:3]:
+        copy.wait()
     for off in range(27):
         block, cols = off // 4, slice(off % 4 * C, (off % 4 + 1) * C)
         flat[off * C : off * C + C // 2] = moments[2 * block, :, cols]
@@ -328,19 +344,23 @@
     gconv[...] = (product * conv_scale).reshape(27, C, C)
     gmix[...] = (jnp.dot(turned, high, preferred_element_type=F32)
                  + jnp.dot(turned, low, preferred_element_type=F32)) * mix_scale
+    for copy in copies[3:]:
+        copy.wait()
 
 
 def local(feats, tile_weight, tile_atom, tile_cell, tile_live, w_mix, conv_w, cotangent):
     vmem = pl.BlockSpec(memory_space=pltpu.VMEM)
-    hbm = pl.BlockSpec(memory_space=pl.ANY)
+    hbm = pl.BlockSpec(memory_space=pltpu.HBM)
     dma = pltpu.SemaphoreType.DMA
     field = jax.ShapeDtypeStruct((C, A_DEV), BF16)
     pot, gfe, total = pl.pallas_call(
         kernel,
         out_shape=(field, field, jax.ShapeDtypeStruct((GROUP, C // 2, 128), F32)),
         in_specs=[hbm] * 4 + [pl.BlockSpec(memory_space=pltpu.SMEM)] + [hbm] * 3,
-        out_specs=(vmem, vmem, vmem),
+        out_specs=(hbm, hbm, hbm),
         scratch_shapes=[
+            pltpu.VMEM((C, A_DEV), BF16),
+            pltpu.VMEM((C, A_DEV), BF16),
             pltpu.VMEM((C, A_DEV), BF16),
             pltpu.VMEM((C, A_DEV), BF16),
             pltpu.VMEM((27, C, C), BF16),
@@ -350,8 +370,8 @@
             pltpu.VMEM((8, 128), jnp.int32),
             pltpu.SMEM((8, 128), jnp.int32),
             pltpu.VMEM((TILES, TILE_A, TILE_C), BF16),
-            pltpu.VMEM((NAB, 2 * C, TILE_A), BF16),
-            pltpu.VMEM((TILES + 1, 2 * C, TILE_C), F32),
+            pltpu.VMEM((2, NAB, C, TILE_A), BF16),
+            pltpu.VMEM((2, TILES + 1, C, TILE_C), F32),
             pltpu.VMEM((2, 3, 4, C, TILE_C), BF16),
             pltpu.VMEM((2, 3, 4, C, TILE_C), BF16),
             pltpu.VMEM((2, 3, 4, C, TILE_C), BF16),
@@ -363,14 +383,15 @@
             pltpu.VMEM((27 * C, 128), F32),
             pltpu.VMEM((12 * C, TILE_C), F32),
             pltpu.VMEM((3, 12 * C, 6 * C), F32),
-            pltpu.VMEM((2, NB, C, TILE_C), BF16),
-            pltpu.VMEM((TILES + 1, 2 * C, TILE_A), F32),
+            pltpu.VMEM((NB, C, TILE_C), BF16),
+            pltpu.VMEM((NB, C, TILE_C), BF16),
+            pltpu.VMEM((2, TILES + 1, C, TILE_A), F32),
             pltpu.VMEM((GROUP, C // 2, 128), F32),
             pltpu.VMEM((GROUP, C // 2, 128), F32),
             pltpu.VMEM((SLABS // 2, C // 2, 128), F32),
             pltpu.VMEM((C // 2, 128), F32),
             pltpu.VMEM((C // 2, 128), F32),
-            dma((7,)), dma((W_CHUNKS,)), dma((3, 2)), dma((3, 2)), dma((2, 2)), dma((2, 2)), dma((3,)), dma((3,)),
+            dma((7,)), dma((3,)), dma((W_CHUNKS,)), dma((3, 2)), dma((3, 2)), dma((2, 2)), dma((2, 2)), dma((3,)), dma((3,)),
         ],
         compiler_params=pltpu.CompilerParams(
             collective_id=0, has_side_effects=True, vmem_limit_bytes=56 * 2**20,
@@ -379,10 +400,15 @@
     pot, gfe, gconv, gmix = pl.pallas_call(
         finish,
         out_shape=(field, field, jax.ShapeDtypeStruct((27, C, C), F32), jax.ShapeDtypeStruct((C, C), F32)),
-        in_specs=[vmem] * 5,
+        in_specs=[hbm] * 5,
         out_specs=(vmem,) * 4,
-        scratch_shapes=[pltpu.VMEM((27 * C, C), F32)],
-        compiler_params=pltpu.CompilerParams(vmem_limit_bytes=32 * 2**20),
+        scratch_shapes=[
+            pltpu.VMEM((GROUP, C // 2, 128), F32),
+            pltpu.VMEM((C, C), BF16),
+            pltpu.VMEM((27, C, C), BF16),
+            pltpu.VMEM((27 * C, C), F32),
+            dma((5,)),
+        ],
     )(pot, gfe, total, w_mix, conv_w)
     return pot[None], gfe[None], gconv, gmix
 

time: 43.8 us -> 40.8 us (0.932)
  local copies, waits for them, and re-layouts: 2.69 us -> 0 us
    unnamed x10 -> x0, local copies, waits for them, and re-layouts: 2.69 us -> none
    pallas_call x1, Pallas kernels: 38.3 us -> 37.1 us  [local(): pl.pallas_call(kernel, out_shape=(field, field, jax.ShapeDtypeStruct((GRO...]
    pallas_call x1, Pallas kernels: 1.19 us -> 2.33 us  [local(): pl.pallas_call(finish, out_shape=(field, field, jax.ShapeDtypeStruct((27,...]
where the time goes in v3:
time: 40.8 us; the launch traced here: 40.7 us
  Pallas kernels  39.4 us (97%)
  between operations  1.29 us (3%)
    pallas_call x1, Pallas kernels, local(): pl.pallas_call(kernel, out_shape=(field, field, jax.ShapeDtypeStruct((GRO...  37.1 us
    pallas_call x1, Pallas kernels, local(): pl.pallas_call(finish, out_shape=(field, field, jax.ShapeDtypeStruct((27,...  2.33 us

profile of v3, /device:TPU:1, one launch (start us, length us, event | category | flops | bytes accessed | tf_op | source)
XLA Modules:
  0.0 40.7 jit_solution(2951079388735828531)
XLA Ops:
  1.3 37.1 %shard_map.111 = (bf16[32,1536]{1,0:T(8,128)(2,1)}, bf16[32,1536]{1,0:T(8,128)(2,1)}, f32[16,16,128]{2,1,0:T(8,128)}) custom-call(bf16[32,1536]{1,0:T(8,128)(2,1)} %bitcast.6, bf16[96,64,512]{2,1,0:T(8,128)(2,1)} %bitcast.5, s32[1,96]{1,0:T(1,128)} %atom_hbm.1, s32[1,96]{1,0:T(1,128)} %cell_hbm.1, s32[1,1]{1,0:T(1,128)S(6)} %copy.12.live, ...), custom_call_target="tpu_custom_call" | custom-call | tf_op jit(solution)/shard_map/pallas_call | solution.py:356
  38.3 2.3 %shard_map.112 = (bf16[32,1536]{1,0:T(8,128)(2,1)}, bf16[32,1536]{1,0:T(8,128)(2,1)}, f32[27,32,32]{2,1,0:T(8,128)}, f32[32,32]{1,0:T(8,128)}) custom-call(bf16[32,1536]{1,0:T(8,128)(2,1)} %get-tuple-element.11.pot_in, bf16[32,1536]{1,0:T(8,128)(2,1)} %get-tuple-element.12.gfe_in, f32[16,16,128]{2,1,0:T(8,128)} %get-tuple-element.13.moments_hbm, ...), custom_call_target="tpu_custom_call" | custom-call | tf_op jit(solution)/shard_map/pallas_call | solution.py:400

commit v4 on v3

--- a/solution.py
+++ b/solution.py
@@ -23,7 +23,6 @@
 W_CHUNKS = 6
 W_STEP = TILES // W_CHUNKS
 
-GROUP = 16
 UNROLL = 8
 PREV_C, LAST_C, PREV_A, LAST_A, ATOM, CELL = range(6)
 
@@ -36,17 +35,15 @@
 def kernel(
     feats_hbm, w_hbm, atom_hbm, cell_hbm, live, mix_hbm, conv_hbm, cot_hbm,
     pot, gfe, gout,
-    pot_v, gfe_v, feats, cot, conv, mix, atom_v, cell_v, idx_v, idx,
+    feats, cot, conv, mix, atom_v, cell_v, idx_v, idx,
     w, src, acc, snd_dn, snd_up, rcv_lo, rcv_hi, shifted, dside, toep1, toep2, rep1, prod, gw,
     win0, win1, cacc, gp, rs1, rs2, piece, fin,
-    in_sem, out_sem, w_sem, h_send, h_recv, p_send, p_recv, g_send, g_recv,
+    in_sem, w_sem, h_send, h_recv, p_send, p_recv, g_send, g_recv,
 ):
     slab = lax.axis_index("slab")
     rep = lax.axis_index("rep")
-    chip, core = slab // 2, lax.rem(slab, 2)
     up = lax.rem(slab + 1, SLABS)
     down = lax.rem(slab + SLABS - 1, SLABS)
-    member = rep * 2 + core
 
     small = []
     pairs = ((cell_hbm, cell_v), (atom_hbm, atom_v), (feats_hbm, feats), (mix_hbm, mix),
@@ -60,15 +57,13 @@
         loads.append(pltpu.make_async_copy(w_hbm.at[part], w.at[part], w_sem.at[k]))
         loads[-1].start()
 
-    def plane_mate(k):
-        other = lax.rem(member + k, GROUP)
-        return {"rep": other // 2, "slab": chip * 2 + lax.rem(other, 2)}
-
-    def row_mate(k):
-        return {"slab": lax.rem(chip + k, SLABS // 2) * 2 + core}
-
-    mates = [plane_mate(k) for k in range(1, GROUP)] + [row_mate(k) for k in range(1, SLABS // 2)]
-    mates += [{"slab": up}, {"slab": down}]
+    def slab_mate(k):
+        return {"slab": lax.rem(slab + k, SLABS)}
+
+    def rep_mate(k):
+        return {"rep": lax.rem(rep + k, REPS)}
+
+    mates = [slab_mate(k) for k in range(1, SLABS)] + [rep_mate(k) for k in range(1, REPS)]
     barrier = pltpu.get_barrier_semaphore()
     for mate in mates:
         pl.semaphore_signal(barrier, inc=1, device_id=mate, device_id_type=MESH)
@@ -180,6 +175,8 @@
     first_x = lax.rem(spot, GX) == 0
     last_x = lax.rem(spot, GX) == GX - 1
 
+    low_half = spot[:C] < GX
+
     def next_x(v):
         return jnp.where(last_x, pltpu.roll(v, GX - 1, 1), pltpu.roll(v, 127, 1))
 
@@ -192,8 +189,11 @@
             [acc[f, idx[LAST_C, (p + 1) * 4 + q]] + got[q].astype(F32) for q in range(4)], axis=1)
         own = slice(p * C, (p + 1) * C)
         shifted[f, 1, own] = plane.astype(BF16)
-        shifted[f, 0, own] = pltpu.roll(plane, GX, 1).astype(BF16)
-        shifted[f, 2, own] = pltpu.roll(plane, CELLS - GX, 1).astype(BF16)
+        turned = [pltpu.roll(plane[:, k * 128 : (k + 1) * 128], GX, 1) for k in range(16)]
+        for k in range(16):
+            cols = slice(k * 128, (k + 1) * 128)
+            shifted[f, 0, own, cols] = jnp.where(low_half, turned[k - 1], turned[k]).astype(BF16)
+            shifted[f, 2, own, cols] = jnp.where(low_half, turned[k], turned[(k + 1) % 16]).astype(BF16)
 
     phis = []
     win = (win0, win1)
@@ -230,25 +230,20 @@
     for k in range(16):
         cols = slice(k * 128, (k + 1) * 128)
         v = shifted[1, 1, C : 5 * C, cols].astype(F32)
-        dside[:128, cols] = next_x(v).astype(BF16)
-        dside[128:256, cols] = shifted[1, 1, C : 5 * C, cols]
-        dside[256:, cols] = prev_x(v).astype(BF16)
+        for dx, moved in enumerate((next_x(v), v, prev_x(v))):
+            for z in range(ZD):
+                dside[z, dx * C : (dx + 1) * C, cols] = moved[z * C : (z + 1) * C].astype(BF16)
     for dy in range(3):
-        gw[dy] = lax.dot_general(dside[...], shifted[0, dy], NT, preferred_element_type=F32)
-    for off in range(27):
-        dz, dy, dx = off // 9, off // 3 % 3, off % 3
         total = None
-        for zo in range(ZD):
-            rows = slice((dx * 4 + zo) * C, (dx * 4 + zo + 1) * C)
-            start = (zo + dz) * C
-            part = gw[dy, rows, start : start + C]
+        for z in range(ZD):
+            part = lax.dot_general(dside[z], shifted[0, dy, z * C : (z + 3) * C], NT, preferred_element_type=F32)
             total = part if total is None else total + part
-        block, cols = off // 4, slice(off % 4 * C, (off % 4 + 1) * C)
-        gp[2 * block, :, cols] = total[: C // 2]
-        gp[2 * block + 1, :, cols] = total[C // 2 :]
-    gp[13, :, 3 * C :] = jnp.zeros((C // 2, C), F32)
-    gp[12, :, 3 * C :] = jnp.zeros((C // 2, C), F32)
-    gp[14:] = jnp.zeros((2, C // 2, 128), F32)
+        gw[:, dy * 3 * C : (dy + 1) * 3 * C] = total
+    for half in range(2):
+        gp[half * 6 : (half + 1) * 6] = gw[:, half * 128 : (half + 1) * 128].reshape(6, C // 2, 128)
+    gp[12:] = jnp.zeros((4, C // 2, 128), F32)
+    for dx in range(3):
+        gp[12:14, :, dx * C : (dx + 1) * C] = gw[dx * C : (dx + 1) * C, 256:].reshape(2, C // 2, C)
 
     def give(source, target, phase, mate):
         pltpu.make_async_remote_copy(
@@ -259,11 +254,11 @@
         part = buffer.at[pl.ds(0, count)]
         return pltpu.make_async_remote_copy(
             src_ref=part, dst_ref=part, send_sem=g_send.at[phase], recv_sem=g_recv.at[phase],
-            device_id=plane_mate(1), device_id_type=MESH)
-
-    for k in range(1, GROUP):
-        give(gp.at[lax.rem(member + k, GROUP)], rs1.at[k], 0, plane_mate(k))
-    rs1[0] = gp[member]
+            device_id=slab_mate(1), device_id_type=MESH)
+
+    for k in range(1, SLABS):
+        give(gp.at[lax.rem(slab + k, SLABS)], rs1.at[k], 0, slab_mate(k))
+    rs1[0] = gp[slab]
 
     halos[4].wait_recv()
     halos[5].wait_recv()
@@ -271,11 +266,11 @@
     stack(1, 5)
     convolve(1)
 
-    all_of(rs1, GROUP - 1, 0).wait_recv()
+    all_of(rs1, SLABS - 1, 0).wait_recv()
     piece[...] = jnp.sum(rs1[...], axis=0)
-    for k in range(1, SLABS // 2):
-        give(piece, rs2.at[chip], 1, row_mate(k))
-    rs2[chip] = piece[...]
+    for k in range(1, REPS):
+        give(piece, rs2.at[rep], 1, rep_mate(k))
+    rs2[rep] = piece[...]
 
     def collect(f):
         def body(i, carry):
@@ -287,50 +282,46 @@
             return carry
 
         lax.fori_loop(0, TILES // UNROLL, body, 0)
-        out_v, out = (gfe_v, gfe) if f else (pot_v, pot)
+        out = gfe if f else pot
         for a in range(0, NAB, 2):
             pair = jnp.concatenate([cacc[f, idx[LAST_A, a]], cacc[f, idx[LAST_A, a + 1]]], axis=1)
-            out_v[:, a * TILE_A : (a + 2) * TILE_A] = pair.astype(BF16)
-        copy = pltpu.make_async_copy(out_v, out, out_sem.at[f])
-        copy.start()
-        return copy
+            out[:, a * TILE_A : (a + 2) * TILE_A] = pair.astype(BF16)
 
     phis[0].wait_recv()
     phis[1].wait_recv()
-    outs = [collect(0)]
-
-    all_of(rs2, SLABS // 2 - 1, 1).wait_recv()
+    collect(0)
+
+    all_of(rs2, REPS - 1, 1).wait_recv()
     fin[...] = jnp.sum(rs2[...], axis=0)
-    for k in range(1, GROUP):
-        give(fin, gout.at[member], 2, plane_mate(k))
-    outs.append(pltpu.make_async_copy(fin, gout.at[member], out_sem.at[2]))
-    outs[-1].start()
+    for k in range(1, SLABS):
+        give(fin, gout.at[slab], 2, slab_mate(k))
+    gout[slab] = fin[...]
 
     phis[2].wait_recv()
     phis[3].wait_recv()
-    outs.append(collect(1))
-
-    all_of(rs1, GROUP - 1, 0).wait_send()
-    all_of(rs2, SLABS // 2 - 1, 1).wait_send()
+    collect(1)
+
+    all_of(rs1, SLABS - 1, 0).wait_send()
+    all_of(rs2, REPS - 1, 1).wait_send()
     for copy in halos + phis:
         copy.wait_send()
-    all_of(rs1, GROUP - 1, 2).wait_send()
-    all_of(rs1, GROUP - 1, 2).wait_recv()
-    for copy in outs:
-        copy.wait()
-
-
-def finish(pot_in, gfe_in, moments_hbm, mix_hbm, conv_hbm, pot, gfe, gconv, gmix, moments, mix, conv, flat, sem):
-    pairs = ((moments_hbm, moments), (mix_hbm, mix), (conv_hbm, conv), (pot_in, pot), (gfe_in, gfe))
-    copies = [pltpu.make_async_copy(source, target, sem.at[k]) for k, (source, target) in enumerate(pairs)]
+    all_of(rs1, SLABS - 1, 2).wait_send()
+    all_of(rs1, SLABS - 1, 2).wait_recv()
+
+
+def finish(pot_in, gfe_in, moments, mix_hbm, conv_hbm, pot, gfe, gconv, gmix, mix, conv, flat, sem):
+    copies = [pltpu.make_async_copy(mix_hbm, mix, sem.at[0]), pltpu.make_async_copy(conv_hbm, conv, sem.at[1]),
+              pltpu.make_async_copy(pot_in, pot, sem.at[2]), pltpu.make_async_copy(gfe_in, gfe, sem.at[3])]
     for copy in copies:
         copy.start()
-    for copy in copies[:3]:
-        copy.wait()
     for off in range(27):
-        block, cols = off // 4, slice(off % 4 * C, (off % 4 + 1) * C)
-        flat[off * C : off * C + C // 2] = moments[2 * block, :, cols]
-        flat[off * C + C // 2 : (off + 1) * C] = moments[2 * block + 1, :, cols]
+        dz, dy, dx = off // 9, off // 3 % 3, off % 3
+        group = dy * 3 + dz
+        first, place = (group // 4 * 6 + dx * 2, group % 4) if group < 8 else (12, dx)
+        part = moments[first : first + 2, :, place * C : (place + 1) * C]
+        flat[off * C : (off + 1) * C] = part.reshape(C, C)
+    copies[0].wait()
+    copies[1].wait()
     value = flat[...]
     high = value.astype(BF16)
     low = (value - high.astype(F32)).astype(BF16)
@@ -344,8 +335,8 @@
     gconv[...] = (product * conv_scale).reshape(27, C, C)
     gmix[...] = (jnp.dot(turned, high, preferred_element_type=F32)
                  + jnp.dot(turned, low, preferred_element_type=F32)) * mix_scale
-    for copy in copies[3:]:
-        copy.wait()
+    copies[2].wait()
+    copies[3].wait()
 
 
 def local(feats, tile_weight, tile_atom, tile_cell, tile_live, w_mix, conv_w, cotangent):
@@ -355,12 +346,10 @@
     field = jax.ShapeDtypeStruct((C, A_DEV), BF16)
     pot, gfe, total = pl.pallas_call(
         kernel,
-        out_shape=(field, field, jax.ShapeDtypeStruct((GROUP, C // 2, 128), F32)),
+        out_shape=(pltpu.VMEM((C, A_DEV), BF16), pltpu.VMEM((C, A_DEV), BF16), pltpu.VMEM((SLABS, C // 2, 128), F32)),
         in_specs=[hbm] * 4 + [pl.BlockSpec(memory_space=pltpu.SMEM)] + [hbm] * 3,
-        out_specs=(hbm, hbm, hbm),
+        out_specs=(vmem, vmem, vmem),
         scratch_shapes=[
-            pltpu.VMEM((C, A_DEV), BF16),
-            pltpu.VMEM((C, A_DEV), BF16),
             pltpu.VMEM((C, A_DEV), BF16),
             pltpu.VMEM((C, A_DEV), BF16),
             pltpu.VMEM((27, C, C), BF16),
@@ -377,21 +366,21 @@
             pltpu.VMEM((2, 3, 4, C, TILE_C), BF16),
             pltpu.VMEM((2, 3, 4, C, TILE_C), BF16),
             pltpu.VMEM((2, 3, 6 * C, CELLS), BF16),
-            pltpu.VMEM((12 * C, CELLS), BF16),
+            pltpu.VMEM((ZD, 3 * C, CELLS), BF16),
             pltpu.VMEM((12 * C, 18 * C), BF16),
             pltpu.VMEM((12 * C, 18 * C), BF16),
             pltpu.VMEM((27 * C, 128), F32),
             pltpu.VMEM((12 * C, TILE_C), F32),
-            pltpu.VMEM((3, 12 * C, 6 * C), F32),
+            pltpu.VMEM((3 * C, 9 * C), F32),
             pltpu.VMEM((NB, C, TILE_C), BF16),
             pltpu.VMEM((NB, C, TILE_C), BF16),
             pltpu.VMEM((2, TILES + 1, C, TILE_A), F32),
-            pltpu.VMEM((GROUP, C // 2, 128), F32),
-            pltpu.VMEM((GROUP, C // 2, 128), F32),
-            pltpu.VMEM((SLABS // 2, C // 2, 128), F32),
+            pltpu.VMEM((SLABS, C // 2, 128), F32),
+            pltpu.VMEM((SLABS, C // 2, 128), F32),
+            pltpu.VMEM((REPS, C // 2, 128), F32),
             pltpu.VMEM((C // 2, 128), F32),
             pltpu.VMEM((C // 2, 128), F32),
-            dma((7,)), dma((3,)), dma((W_CHUNKS,)), dma((3, 2)), dma((3, 2)), dma((2, 2)), dma((2, 2)), dma((3,)), dma((3,)),
+            dma((7,)), dma((W_CHUNKS,)), dma((3, 2)), dma((3, 2)), dma((2, 2)), dma((2, 2)), dma((3,)), dma((3,)),
         ],
         compiler_params=pltpu.CompilerParams(
             collective_id=0, has_side_effects=True, vmem_limit_bytes=56 * 2**20,
@@ -400,14 +389,13 @@
     pot, gfe, gconv, gmix = pl.pallas_call(
         finish,
         out_shape=(field, field, jax.ShapeDtypeStruct((27, C, C), F32), jax.ShapeDtypeStruct((C, C), F32)),
-        in_specs=[hbm] * 5,
-        out_specs=(vmem,) * 4,
+        in_specs=[vmem, vmem, vmem, hbm, hbm],
+        out_specs=(hbm, hbm, vmem, vmem),
         scratch_shapes=[
-            pltpu.VMEM((GROUP, C // 2, 128), F32),
             pltpu.VMEM((C, C), BF16),
             pltpu.VMEM((27, C, C), BF16),
             pltpu.VMEM((27 * C, C), F32),
-            dma((5,)),
+            dma((4,)),
         ],
     )(pot, gfe, total, w_mix, conv_w)
     return pot[None], gfe[None], gconv, gmix

time: 40.8 us -> 43.6 us (1.069)
  local copies, waits for them, and re-layouts: 0 us -> 1.92 us
  Pallas kernels: 39.4 us -> 40.2 us
    unnamed x0 -> x6, local copies, waits for them, and re-layouts: none -> 1.92 us
    pallas_call x1, Pallas kernels: 2.33 us -> 3.15 us  [local(): pl.pallas_call(finish, out_shape=(field, field, jax.ShapeDtypeStruct((27,...]
where the time goes in v4:
time: 43.6 us; the launch traced here: 43.5 us
  Pallas kernels  40.2 us (92%)
  local copies, waits for them, and re-layouts  1.92 us (4%)
  between operations  1.3 us (3%)
    pallas_call x1, Pallas kernels, local(): pl.pallas_call(kernel, out_shape=(pltpu.VMEM((C, A_DEV), BF16), pltpu.VME...  37.1 us
    pallas_call x1, Pallas kernels, local(): pl.pallas_call(finish, out_shape=(field, field, jax.ShapeDtypeStruct((27,...  3.15 us
    unnamed x6, local copies, waits for them, and re-layouts  1.92 us

profile of v4, /device:TPU:1, one launch (start us, length us, event | category | flops | bytes accessed | tf_op | source)
XLA Modules:
  0.0 43.5 jit_solution(14305821119642744001)
XLA Ops:
  1.3 37.1 %shard_map.111 = (bf16[32,1536]{1,0:T(8,128)(2,1)S(1)}, bf16[32,1536]{1,0:T(8,128)(2,1)S(1)}, f32[16,16,128]{2,1,0:T(8,128)S(1)}) custom-call(bf16[32,1536]{1,0:T(8,128)(2,1)} %bitcast.6, bf16[96,64,512]{2,1,0:T(8,128)(2,1)} %bitcast.5, s32[1,96]{1,0:T(1,128)} %atom_hbm.1, s32[1,96]{1,0:T(1,128)} %cell_hbm.1, s32[1,1]{1,0:T(1,128)S(6)} %copy.12.live, ...), custom_call_target="tpu_custom_call" | custom-call | tf_op jit(solution)/shard_map/pallas_call | solution.py:347
  38.4 0.0 copy-start
  38.4 0.6 %copy-done = f32[16,16,128]{2,1,0:T(8,128)} copy-done((f32[16,16,128]{2,1,0:T(8,128)}, f32[16,16,128]{2,1,0:T(8,128)S(1)}, u32[]{:S(2)}) %copy-start) | copy-done | bytes 131096
  39.0 0.0 copy-start.1
  39.0 0.6 %copy-done.1 = bf16[32,1536]{1,0:T(8,128)(2,1)} copy-done((bf16[32,1536]{1,0:T(8,128)(2,1)}, bf16[32,1536]{1,0:T(8,128)(2,1)S(1)}, u32[]{:S(2)}) %copy-start.1) | copy-done | bytes 98328
  39.7 0.0 copy-start.2
  39.7 0.6 %copy-done.2 = bf16[32,1536]{1,0:T(8,128)(2,1)} copy-done((bf16[32,1536]{1,0:T(8,128)(2,1)}, bf16[32,1536]{1,0:T(8,128)(2,1)S(1)}, u32[]{:S(2)}) %copy-start.2) | copy-done | bytes 98328
  40.3 3.2 %shard_map.112 = (bf16[32,1536]{1,0:T(8,128)(2,1)}, bf16[32,1536]{1,0:T(8,128)(2,1)}, f32[27,32,32]{2,1,0:T(8,128)}, f32[32,32]{1,0:T(8,128)}) custom-call(bf16[32,1536]{1,0:T(8,128)(2,1)} %copy-done.1, bf16[32,1536]{1,0:T(8,128)(2,1)} %copy-done.2, f32[16,16,128]{2,1,0:T(8,128)} %copy-done, bf16[32,32]{1,0:T(8,128)(2,1)} %mix_hbm.3, ...), custom_call_target="tpu_custom_call" | custom-call | tf_op jit(solution)/shard_map/pallas_call | solution.py:389
Async XLA Ops:
  38.4 0.7 %copy-start = (f32[16,16,128]{2,1,0:T(8,128)}, f32[16,16,128]{2,1,0:T(8,128)S(1)}, u32[]{:S(2)}) copy-start(f32[16,16,128]{2,1,0:T(8,128)S(1)} %get-tuple-element.13.moments) | copy-start | bytes 393220
  39.0 0.6 %copy-start.1 = (bf16[32,1536]{1,0:T(8,128)(2,1)}, bf16[32,1536]{1,0:T(8,128)(2,1)S(1)}, u32[]{:S(2)}) copy-start(bf16[32,1536]{1,0:T(8,128)(2,1)S(1)} %get-tuple-element.11.pot_in) | copy-start | bytes 294916
  39.7 0.6 %copy-start.2 = (bf16[32,1536]{1,0:T(8,128)(2,1)}, bf16[32,1536]{1,0:T(8,128)(2,1)S(1)}, u32[]{:S(2)}) copy-start(bf16[32,1536]{1,0:T(8,128)(2,1)S(1)} %get-tuple-element.12.gfe_in) | copy-start | bytes 294916

commit v5 on v3

--- a/solution.py
+++ b/solution.py
@@ -23,8 +23,9 @@
 W_CHUNKS = 6
 W_STEP = TILES // W_CHUNKS
 
+UNROLL = 8
 GROUP = 16
-UNROLL = 8
+ROW = 8
 PREV_C, LAST_C, PREV_A, LAST_A, ATOM, CELL = range(6)
 
 F32 = jnp.float32
@@ -44,9 +45,9 @@
     slab = lax.axis_index("slab")
     rep = lax.axis_index("rep")
     chip, core = slab // 2, lax.rem(slab, 2)
+    member = rep * 2 + core
     up = lax.rem(slab + 1, SLABS)
     down = lax.rem(slab + SLABS - 1, SLABS)
-    member = rep * 2 + core
 
     small = []
     pairs = ((cell_hbm, cell_v), (atom_hbm, atom_v), (feats_hbm, feats), (mix_hbm, mix),
@@ -65,9 +66,9 @@
         return {"rep": other // 2, "slab": chip * 2 + lax.rem(other, 2)}
 
     def row_mate(k):
-        return {"slab": lax.rem(chip + k, SLABS // 2) * 2 + core}
-
-    mates = [plane_mate(k) for k in range(1, GROUP)] + [row_mate(k) for k in range(1, SLABS // 2)]
+        return {"slab": lax.rem(chip + k, ROW) * 2 + core}
+
+    mates = [plane_mate(k) for k in range(1, GROUP)] + [row_mate(k) for k in range(1, ROW)]
     mates += [{"slab": up}, {"slab": down}]
     barrier = pltpu.get_barrier_semaphore()
     for mate in mates:
@@ -180,6 +181,8 @@
     first_x = lax.rem(spot, GX) == 0
     last_x = lax.rem(spot, GX) == GX - 1
 
+    low_half = spot[:C] < GX
+
     def next_x(v):
         return jnp.where(last_x, pltpu.roll(v, GX - 1, 1), pltpu.roll(v, 127, 1))
 
@@ -192,13 +195,16 @@
             [acc[f, idx[LAST_C, (p + 1) * 4 + q]] + got[q].astype(F32) for q in range(4)], axis=1)
         own = slice(p * C, (p + 1) * C)
         shifted[f, 1, own] = plane.astype(BF16)
-        shifted[f, 0, own] = pltpu.roll(plane, GX, 1).astype(BF16)
-        shifted[f, 2, own] = pltpu.roll(plane, CELLS - GX, 1).astype(BF16)
+        turned = [pltpu.roll(plane[:, k * 128 : (k + 1) * 128], GX, 1) for k in range(16)]
+        for k in range(16):
+            cols = slice(k * 128, (k + 1) * 128)
+            shifted[f, 0, own, cols] = jnp.where(low_half, turned[k - 1], turned[k]).astype(BF16)
+            shifted[f, 2, own, cols] = jnp.where(low_half, turned[k], turned[(k + 1) % 16]).astype(BF16)
 
     phis = []
     win = (win0, win1)
 
-    def convolve(f):
+    def convolve(f, before_send):
         toep = toep2 if f else toep1
         for q in range(4):
             cols = slice(q * TILE_C, (q + 1) * TILE_C)
@@ -210,6 +216,7 @@
                 phi = (mid + prev_x(low) + next_x(high)).astype(BF16)
                 for z in range(ZD):
                     win[f][(z + 2) * 4 + q, :, part] = phi[z * C : (z + 1) * C]
+        before_send()
         for side, (start, land, to) in enumerate(((8, 24, down), (16, 0, up))):
             phis.append(pltpu.make_async_remote_copy(
                 src_ref=win[f].at[pl.ds(start, 8)], dst_ref=win[f].at[pl.ds(land, 8)],
@@ -221,7 +228,7 @@
     halos[1].wait_recv()
     for p in range(6):
         stack(0, p)
-    convolve(0)
+    convolve(0, lambda: None)
 
     halos[2].wait_recv()
     halos[3].wait_recv()
@@ -230,25 +237,20 @@
     for k in range(16):
         cols = slice(k * 128, (k + 1) * 128)
         v = shifted[1, 1, C : 5 * C, cols].astype(F32)
-        dside[:128, cols] = next_x(v).astype(BF16)
-        dside[128:256, cols] = shifted[1, 1, C : 5 * C, cols]
-        dside[256:, cols] = prev_x(v).astype(BF16)
+        for dx, moved in enumerate((next_x(v), v, prev_x(v))):
+            for z in range(ZD):
+                dside[z, dx * C : (dx + 1) * C, cols] = moved[z * C : (z + 1) * C].astype(BF16)
     for dy in range(3):
-        gw[dy] = lax.dot_general(dside[...], shifted[0, dy], NT, preferred_element_type=F32)
-    for off in range(27):
-        dz, dy, dx = off // 9, off // 3 % 3, off % 3
         total = None
-        for zo in range(ZD):
-            rows = slice((dx * 4 + zo) * C, (dx * 4 + zo + 1) * C)
-            start = (zo + dz) * C
-            part = gw[dy, rows, start : start + C]
+        for z in range(ZD):
+            part = lax.dot_general(dside[z], shifted[0, dy, z * C : (z + 3) * C], NT, preferred_element_type=F32)
             total = part if total is None else total + part
-        block, cols = off // 4, slice(off % 4 * C, (off % 4 + 1) * C)
-        gp[2 * block, :, cols] = total[: C // 2]
-        gp[2 * block + 1, :, cols] = total[C // 2 :]
-    gp[13, :, 3 * C :] = jnp.zeros((C // 2, C), F32)
-    gp[12, :, 3 * C :] = jnp.zeros((C // 2, C), F32)
-    gp[14:] = jnp.zeros((2, C // 2, 128), F32)
+        gw[:, dy * 3 * C : (dy + 1) * 3 * C] = total
+    for half in range(2):
+        gp[half * 6 : (half + 1) * 6] = gw[:, half * 128 : (half + 1) * 128].reshape(6, C // 2, 128)
+    gp[12:] = jnp.zeros((4, C // 2, 128), F32)
+    for dx in range(3):
+        gp[12:14, :, dx * C : (dx + 1) * C] = gw[dx * C : (dx + 1) * C, 256:].reshape(2, C // 2, C)
 
     def give(source, target, phase, mate):
         pltpu.make_async_remote_copy(
@@ -265,17 +267,18 @@
         give(gp.at[lax.rem(member + k, GROUP)], rs1.at[k], 0, plane_mate(k))
     rs1[0] = gp[member]
 
+    def middle():
+        all_of(rs1, GROUP - 1, 0).wait_recv()
+        piece[...] = jnp.sum(rs1[...], axis=0)
+        for k in range(1, ROW):
+            give(piece, rs2.at[chip], 1, row_mate(k))
+        rs2[chip] = piece[...]
+
     halos[4].wait_recv()
     halos[5].wait_recv()
     stack(1, 0)
     stack(1, 5)
-    convolve(1)
-
-    all_of(rs1, GROUP - 1, 0).wait_recv()
-    piece[...] = jnp.sum(rs1[...], axis=0)
-    for k in range(1, SLABS // 2):
-        give(piece, rs2.at[chip], 1, row_mate(k))
-    rs2[chip] = piece[...]
+    convolve(1, middle)
 
     def collect(f):
         def body(i, carry):
@@ -299,7 +302,7 @@
     phis[1].wait_recv()
     outs = [collect(0)]
 
-    all_of(rs2, SLABS // 2 - 1, 1).wait_recv()
+    all_of(rs2, ROW - 1, 1).wait_recv()
     fin[...] = jnp.sum(rs2[...], axis=0)
     for k in range(1, GROUP):
         give(fin, gout.at[member], 2, plane_mate(k))
@@ -311,7 +314,7 @@
     outs.append(collect(1))
 
     all_of(rs1, GROUP - 1, 0).wait_send()
-    all_of(rs2, SLABS // 2 - 1, 1).wait_send()
+    all_of(rs2, ROW - 1, 1).wait_send()
     for copy in halos + phis:
         copy.wait_send()
     all_of(rs1, GROUP - 1, 2).wait_send()
@@ -328,9 +331,11 @@
     for copy in copies[:3]:
         copy.wait()
     for off in range(27):
-        block, cols = off // 4, slice(off % 4 * C, (off % 4 + 1) * C)
-        flat[off * C : off * C + C // 2] = moments[2 * block, :, cols]
-        flat[off * C + C // 2 : (off + 1) * C] = moments[2 * block + 1, :, cols]
+        dz, dy, dx = off // 9, off // 3 % 3, off % 3
+        group = dy * 3 + dz
+        first, place = (group // 4 * 6 + dx * 2, group % 4) if group < 8 else (12, dx)
+        part = moments[first : first + 2, :, place * C : (place + 1) * C]
+        flat[off * C : (off + 1) * C] = part.reshape(C, C)
     value = flat[...]
     high = value.astype(BF16)
     low = (value - high.astype(F32)).astype(BF16)
@@ -377,18 +382,18 @@
             pltpu.VMEM((2, 3, 4, C, TILE_C), BF16),
             pltpu.VMEM((2, 3, 4, C, TILE_C), BF16),
             pltpu.VMEM((2, 3, 6 * C, CELLS), BF16),
-            pltpu.VMEM((12 * C, CELLS), BF16),
+            pltpu.VMEM((ZD, 3 * C, CELLS), BF16),
             pltpu.VMEM((12 * C, 18 * C), BF16),
             pltpu.VMEM((12 * C, 18 * C), BF16),
             pltpu.VMEM((27 * C, 128), F32),
             pltpu.VMEM((12 * C, TILE_C), F32),
-            pltpu.VMEM((3, 12 * C, 6 * C), F32),
+            pltpu.VMEM((3 * C, 9 * C), F32),
             pltpu.VMEM((NB, C, TILE_C), BF16),
             pltpu.VMEM((NB, C, TILE_C), BF16),
             pltpu.VMEM((2, TILES + 1, C, TILE_A), F32),
             pltpu.VMEM((GROUP, C // 2, 128), F32),
             pltpu.VMEM((GROUP, C // 2, 128), F32),
-            pltpu.VMEM((SLABS // 2, C // 2, 128), F32),
+            pltpu.VMEM((ROW, C // 2, 128), F32),
             pltpu.VMEM((C // 2, 128), F32),
             pltpu.VMEM((C // 2, 128), F32),
             dma((7,)), dma((3,)), dma((W_CHUNKS,)), dma((3, 2)), dma((3, 2)), dma((2, 2)), dma((2, 2)), dma((3,)), dma((3,)),

time: 40.8 us -> 41.1 us (level)
  no operation moved by 1% of the time
where the time goes in v5:
time: 41.1 us; the launch traced here: 41 us
  Pallas kernels  39.7 us (97%)
  between operations  1.29 us (3%)
    pallas_call x1, Pallas kernels, local(): pl.pallas_call(kernel, out_shape=(field, field, jax.ShapeDtypeStruct((GRO...  37.3 us
    pallas_call x1, Pallas kernels, local(): pl.pallas_call(finish, out_shape=(field, field, jax.ShapeDtypeStruct((27,...  2.33 us

profile of v5, /device:TPU:1, one launch (start us, length us, event | category | flops | bytes accessed | tf_op | source)
XLA Modules:
  0.0 41.0 jit_solution(15639494053817596602)
XLA Ops:
  1.3 37.3 %shard_map.111 = (bf16[32,1536]{1,0:T(8,128)(2,1)}, bf16[32,1536]{1,0:T(8,128)(2,1)}, f32[16,16,128]{2,1,0:T(8,128)}) custom-call(bf16[32,1536]{1,0:T(8,128)(2,1)} %bitcast.6, bf16[96,64,512]{2,1,0:T(8,128)(2,1)} %bitcast.5, s32[1,96]{1,0:T(1,128)} %atom_hbm.1, s32[1,96]{1,0:T(1,128)} %cell_hbm.1, s32[1,1]{1,0:T(1,128)S(6)} %copy.12.live, ...), custom_call_target="tpu_custom_call" | custom-call | tf_op jit(solution)/shard_map/pallas_call | solution.py:361
  38.6 2.3 %shard_map.112 = (bf16[32,1536]{1,0:T(8,128)(2,1)}, bf16[32,1536]{1,0:T(8,128)(2,1)}, f32[27,32,32]{2,1,0:T(8,128)}, f32[32,32]{1,0:T(8,128)}) custom-call(bf16[32,1536]{1,0:T(8,128)(2,1)} %get-tuple-element.11.pot_in, bf16[32,1536]{1,0:T(8,128)(2,1)} %get-tuple-element.12.gfe_in, f32[16,16,128]{2,1,0:T(8,128)} %get-tuple-element.13.moments_hbm, ...), custom_call_target="tpu_custom_call" | custom-call | tf_op jit(solution)/shard_map/pallas_call | solution.py:405

commit v6 on v5

--- a/solution.py
+++ b/solution.py
@@ -20,10 +20,10 @@
 CELLS = GY * GX
 SLABS = 16
 REPS = 8
-W_CHUNKS = 6
+W_CHUNKS = 4
 W_STEP = TILES // W_CHUNKS
 
-UNROLL = 8
+UNROLL = 24
 GROUP = 16
 ROW = 8
 PREV_C, LAST_C, PREV_A, LAST_A, ATOM, CELL = range(6)
@@ -68,8 +68,9 @@
     def row_mate(k):
         return {"slab": lax.rem(chip + k, ROW) * 2 + core}
 
-    mates = [plane_mate(k) for k in range(1, GROUP)] + [row_mate(k) for k in range(1, ROW)]
-    mates += [{"slab": up}, {"slab": down}]
+    plane_mates = [plane_mate(k) for k in range(1, GROUP)]
+    row_mates = [row_mate(k) for k in range(1, ROW)]
+    mates = plane_mates + row_mates + [{"slab": up}, {"slab": down}]
     barrier = pltpu.get_barrier_semaphore()
     for mate in mates:
         pl.semaphore_signal(barrier, inc=1, device_id=mate, device_id_type=MESH)
@@ -204,7 +205,7 @@
     phis = []
     win = (win0, win1)
 
-    def convolve(f, before_send):
+    def convolve(f):
         toep = toep2 if f else toep1
         for q in range(4):
             cols = slice(q * TILE_C, (q + 1) * TILE_C)
@@ -216,7 +217,6 @@
                 phi = (mid + prev_x(low) + next_x(high)).astype(BF16)
                 for z in range(ZD):
                     win[f][(z + 2) * 4 + q, :, part] = phi[z * C : (z + 1) * C]
-        before_send()
         for side, (start, land, to) in enumerate(((8, 24, down), (16, 0, up))):
             phis.append(pltpu.make_async_remote_copy(
                 src_ref=win[f].at[pl.ds(start, 8)], dst_ref=win[f].at[pl.ds(land, 8)],
@@ -228,7 +228,7 @@
     halos[1].wait_recv()
     for p in range(6):
         stack(0, p)
-    convolve(0, lambda: None)
+    convolve(0)
 
     halos[2].wait_recv()
     halos[3].wait_recv()
@@ -261,24 +261,23 @@
         part = buffer.at[pl.ds(0, count)]
         return pltpu.make_async_remote_copy(
             src_ref=part, dst_ref=part, send_sem=g_send.at[phase], recv_sem=g_recv.at[phase],
-            device_id=plane_mate(1), device_id_type=MESH)
+            device_id=plane_mates[0], device_id_type=MESH)
 
     for k in range(1, GROUP):
-        give(gp.at[lax.rem(member + k, GROUP)], rs1.at[k], 0, plane_mate(k))
+        give(gp.at[lax.rem(member + k, GROUP)], rs1.at[k], 0, plane_mates[k - 1])
     rs1[0] = gp[member]
-
-    def middle():
-        all_of(rs1, GROUP - 1, 0).wait_recv()
-        piece[...] = jnp.sum(rs1[...], axis=0)
-        for k in range(1, ROW):
-            give(piece, rs2.at[chip], 1, row_mate(k))
-        rs2[chip] = piece[...]
 
     halos[4].wait_recv()
     halos[5].wait_recv()
     stack(1, 0)
     stack(1, 5)
-    convolve(1, middle)
+    convolve(1)
+
+    all_of(rs1, GROUP - 1, 0).wait_recv()
+    piece[...] = jnp.sum(rs1[...], axis=0)
+    for k in range(1, ROW):
+        give(piece, rs2.at[chip], 1, row_mates[k - 1])
+    rs2[chip] = piece[...]
 
     def collect(f):
         def body(i, carry):
@@ -305,7 +304,7 @@
     all_of(rs2, ROW - 1, 1).wait_recv()
     fin[...] = jnp.sum(rs2[...], axis=0)
     for k in range(1, GROUP):
-        give(fin, gout.at[member], 2, plane_mate(k))
+        give(fin, gout.at[member], 2, plane_mates[k - 1])
     outs.append(pltpu.make_async_copy(fin, gout.at[member], out_sem.at[2]))
     outs[-1].start()
 

time: 41.1 us -> 40.8 us (level)
  no operation moved by 1% of the time
where the time goes in v6:
time: 40.8 us; the launch traced here: 40.7 us
  Pallas kernels  39.4 us (97%)
  between operations  1.29 us (3%)
    pallas_call x1, Pallas kernels, local(): pl.pallas_call(kernel, out_shape=(field, field, jax.ShapeDtypeStruct((GRO...  37.1 us
    pallas_call x1, Pallas kernels, local(): pl.pallas_call(finish, out_shape=(field, field, jax.ShapeDtypeStruct((27,...  2.33 us

profile of v6, /device:TPU:1, one launch (start us, length us, event | category | flops | bytes accessed | tf_op | source)
XLA Modules:
  0.0 40.7 jit_solution(6472799280997721558)
XLA Ops:
  1.3 37.1 %shard_map.111 = (bf16[32,1536]{1,0:T(8,128)(2,1)}, bf16[32,1536]{1,0:T(8,128)(2,1)}, f32[16,16,128]{2,1,0:T(8,128)}) custom-call(bf16[32,1536]{1,0:T(8,128)(2,1)} %bitcast.6, bf16[96,64,512]{2,1,0:T(8,128)(2,1)} %bitcast.5, s32[1,96]{1,0:T(1,128)} %atom_hbm.1, s32[1,96]{1,0:T(1,128)} %cell_hbm.1, s32[1,1]{1,0:T(1,128)S(6)} %copy.12.live, ...), custom_call_target="tpu_custom_call" | custom-call | tf_op jit(solution)/shard_map/pallas_call | solution.py:360
  38.4 2.3 %shard_map.112 = (bf16[32,1536]{1,0:T(8,128)(2,1)}, bf16[32,1536]{1,0:T(8,128)(2,1)}, f32[27,32,32]{2,1,0:T(8,128)}, f32[32,32]{1,0:T(8,128)}) custom-call(bf16[32,1536]{1,0:T(8,128)(2,1)} %get-tuple-element.11.pot_in, bf16[32,1536]{1,0:T(8,128)(2,1)} %get-tuple-element.12.gfe_in, f32[16,16,128]{2,1,0:T(8,128)} %get-tuple-element.13.moments_hbm, ...), custom_call_target="tpu_custom_call" | custom-call | tf_op jit(solution)/shard_map/pallas_call | solution.py:404

commit v7 on v6

--- a/solution.py
+++ b/solution.py
@@ -26,6 +26,8 @@
 UNROLL = 24
 GROUP = 16
 ROW = 8
+GROUP_STEPS = (10, 11, 9, 8, 6, 14, 7, 5, 13, 15, 4, 12, 3, 2, 1)
+ROW_STEPS = (6, 2, 5, 3, 7, 1, 4)
 PREV_C, LAST_C, PREV_A, LAST_A, ATOM, CELL = range(6)
 
 F32 = jnp.float32
@@ -263,7 +265,7 @@
             src_ref=part, dst_ref=part, send_sem=g_send.at[phase], recv_sem=g_recv.at[phase],
             device_id=plane_mates[0], device_id_type=MESH)
 
-    for k in range(1, GROUP):
+    for k in GROUP_STEPS:
         give(gp.at[lax.rem(member + k, GROUP)], rs1.at[k], 0, plane_mates[k - 1])
     rs1[0] = gp[member]
 
@@ -275,7 +277,7 @@
 
     all_of(rs1, GROUP - 1, 0).wait_recv()
     piece[...] = jnp.sum(rs1[...], axis=0)
-    for k in range(1, ROW):
+    for k in ROW_STEPS:
         give(piece, rs2.at[chip], 1, row_mates[k - 1])
     rs2[chip] = piece[...]
 
@@ -303,7 +305,7 @@
 
     all_of(rs2, ROW - 1, 1).wait_recv()
     fin[...] = jnp.sum(rs2[...], axis=0)
-    for k in range(1, GROUP):
+    for k in GROUP_STEPS:
         give(fin, gout.at[member], 2, plane_mates[k - 1])
     outs.append(pltpu.make_async_copy(fin, gout.at[member], out_sem.at[2]))
     outs[-1].start()
@@ -327,8 +329,11 @@
     copies = [pltpu.make_async_copy(source, target, sem.at[k]) for k, (source, target) in enumerate(pairs)]
     for copy in copies:
         copy.start()
-    for copy in copies[:3]:
-        copy.wait()
+    copies[1].wait()
+    copies[2].wait()
+    mixing = mix[...]
+    turned = conv[...].reshape(27 * C, C).astype(F32).T.astype(BF16)
+    copies[0].wait()
     for off in range(27):
         dz, dy, dx = off // 9, off // 3 % 3, off % 3
         group = dy * 3 + dz
@@ -338,8 +343,6 @@
     value = flat[...]
     high = value.astype(BF16)
     low = (value - high.astype(F32)).astype(BF16)
-    mixing = mix[...]
-    turned = conv[...].reshape(27 * C, C).astype(F32).T.astype(BF16)
     devices = REPS * SLABS
     conv_scale = 1.0 / math.sqrt(devices * ZD * GY * GX)
     mix_scale = 1.0 / math.sqrt(devices * A_DEV)

time: 40.8 us -> 40.9 us (level)
  no operation moved by 1% of the time
where the time goes in v7:
time: 40.9 us; the launch traced here: 40.8 us
  Pallas kernels  39.5 us (97%)
  between operations  1.29 us (3%)
    pallas_call x1, Pallas kernels, local(): pl.pallas_call(kernel, out_shape=(field, field, jax.ShapeDtypeStruct((GRO...  37 us
    pallas_call x1, Pallas kernels, local(): pl.pallas_call(finish, out_shape=(field, field, jax.ShapeDtypeStruct((27,...  2.44 us

profile of v7, /device:TPU:1, one launch (start us, length us, event | category | flops | bytes accessed | tf_op | source)
XLA Modules:
  0.0 40.8 jit_solution(2189380863850415784)
XLA Ops:
  1.3 37.0 %shard_map.111 = (bf16[32,1536]{1,0:T(8,128)(2,1)}, bf16[32,1536]{1,0:T(8,128)(2,1)}, f32[16,16,128]{2,1,0:T(8,128)}) custom-call(bf16[32,1536]{1,0:T(8,128)(2,1)} %bitcast.6, bf16[96,64,512]{2,1,0:T(8,128)(2,1)} %bitcast.5, s32[1,96]{1,0:T(1,128)} %atom_hbm.1, s32[1,96]{1,0:T(1,128)} %cell_hbm.1, s32[1,1]{1,0:T(1,128)S(6)} %copy.12.live, ...), custom_call_target="tpu_custom_call" | custom-call | tf_op jit(solution)/shard_map/pallas_call | solution.py:363
  38.3 2.4 %shard_map.112 = (bf16[32,1536]{1,0:T(8,128)(2,1)}, bf16[32,1536]{1,0:T(8,128)(2,1)}, f32[27,32,32]{2,1,0:T(8,128)}, f32[32,32]{1,0:T(8,128)}) custom-call(bf16[32,1536]{1,0:T(8,128)(2,1)} %get-tuple-element.11.pot_in, bf16[32,1536]{1,0:T(8,128)(2,1)} %get-tuple-element.12.gfe_in, f32[16,16,128]{2,1,0:T(8,128)} %get-tuple-element.13.moments_hbm, ...), custom_call_target="tpu_custom_call" | custom-call | tf_op jit(solution)/shard_map/pallas_call | solution.py:407
